TPU v7x, 32 devices: a whole 2x2x4 slice. The times are simulated.
32 devices in a mesh: groups: 2 (over x), blk: 16 (over z, y, core).
Axes of the slice: x: 2, y: 2, z: 4, core: 2. Of those that a mesh axis runs over, the one named last changes fastest.
Arguments:
- state_now: float32 [5, 64, 16384], P(None, None, ('groups', 'blk')), parts along dimension 2, may hold values from -6 to 6
- time_source: float32 [5, 64, 16384], P(None, None, ('groups', 'blk')), parts along dimension 2, may hold values from -6 to 6
- viscosity: float32 [64, 16384], P(None, ('groups', 'blk')), parts along dimension 1, may hold values from 0.05 to 0.5
- advection: float32 [5], replicated, may hold values from 0.2 to 1
- coupling: float32 [5, 5], replicated, may hold values from -2.5 to 2.5
- owner_list: int32 [16384, 1], P(('groups', 'blk')), parts along dimension 0, may hold values from 0 to 15; in each aligned block of 512 rows (0 to 511, 512 to 1023, ...) at most 64 rows name the same one
- owner_offset: int32 [16384], P(('groups', 'blk')), parts along dimension 0, may hold values from 0 to 510
- intersection_weight: float32 [16384], P(('groups', 'blk')), parts along dimension 0, may hold values from 0 to 1
- phase_index: int32 [32], P(('groups', 'blk')), parts along dimension 0, may hold values from 0 to 511
Outputs:
- state_next: float32 [5, 64, 16384], P(None, None, ('groups', 'blk')), parts along dimension 2
There are 2 independent parts, one for each index of `groups`. A program takes and returns all parts, laid end to end along the dimension named above; an argument that names none is the same for every part. Nothing has to cross between parts.
Inputs may be any that keep to these rules, and one draw needn't show every extreme that they name: `owner_list`: within the 512 ghost cells of one block, no owner block is named more than 64 times, a bound that some block reaches.
All inputs are finite; a program needn't handle non-finite values.
Results may differ from a plain program's by a relative error of at most 0.0001.
Values sent between devices are 32-bit elements; how exact they have to be, the bound alone decides.
No kernel may reach another device: no remote copies, remote signals or barrier semaphores. Data moves between devices by JAX's collectives and lax.ppermute only.
A program may use at most 64 MiB of HBM per device.

v0:
```python
import math

import jax
import jax.numpy as jnp
from jax import lax
from jax.sharding import PartitionSpec as P

HARM = 8
PHASES = 512
LAG = 37
ITERS = 4


pseudo_step = 0.2


def stencil(block, lower, upper, viscosity, advection, coupling):
    column = jnp.concatenate([lower[:, None, :], block, upper[:, None, :]], axis=1)
    padded = jnp.pad(block, ((0, 0), (0, 0), (1, 1)))
    before = padded[:, :, :-2]
    after = padded[:, :, 2:]
    diffuse = 4.0 * block - column[:, :-2, :] - column[:, 2:, :] - before - after
    mixing = jnp.einsum("cd,djn->cjn", coupling, block, precision=lax.Precision.HIGHEST)
    return advection[:, None, None] * (block - before) + viscosity[None] * diffuse + mixing


def update(block, source, lower, upper, viscosity, advection, coupling):
    change = 1.5 * block + source + stencil(block, lower, upper, viscosity, advection, coupling)
    return block - pseudo_step * change


def harmonic_terms(phase_index, count):
    angle = phase_index.astype(jnp.float32) * (2.0 * math.pi / PHASES)
    orders = jnp.arange(1, HARM + 1, dtype=jnp.float32)
    product = angle[:, None] * orders[None, :]
    ones = jnp.ones_like(angle)[:, None]
    return jnp.concatenate([ones, 2.0 * jnp.cos(product), 2.0 * jnp.sin(product)], axis=1) / count


def harmonic_basis(phase_index):
    angle = (phase_index.astype(jnp.float32) + LAG) * (2.0 * math.pi / PHASES)
    orders = jnp.arange(1, HARM + 1, dtype=jnp.float32)
    product = angle[:, None] * orders[None, :]
    ones = jnp.ones_like(angle)[:, None]
    return jnp.concatenate([ones, jnp.cos(product), jnp.sin(product)], axis=1)


def accumulate(pieces):
    faces, weights = pieces
    return jnp.einsum("kh,kcn->hcn", weights, faces, precision=lax.Precision.HIGHEST)


def per_device(
    state_now,
    time_source,
    viscosity,
    advection,
    coupling,
    owner_list,
    owner_offset,
    intersection_weight,
    phase_index,
):
    devices = lax.axis_size("blk")
    fields = state_now.shape[0]
    width = state_now.shape[2]
    capacity = 2 * width // devices
    owners = owner_list[:, 0]
    member = (owners[:, None] == jnp.arange(devices, dtype=jnp.int32)[None, :]).astype(jnp.int32)
    ranking = jnp.sum((jnp.cumsum(member, axis=0) - 1) * member, axis=1)
    slot_index = owners * capacity + ranking
    wanted = jnp.zeros((devices * capacity,), jnp.int32).at[slot_index].set(owner_offset)
    served = lax.all_to_all(wanted, "blk", split_axis=0, concat_axis=0, tiled=True)
    own_terms = harmonic_terms(phase_index, devices)
    own_basis = harmonic_basis(phase_index)[0]
    state = state_now
    for iteration in range(ITERS):
        top_face = state[:, -1, :]
        pairs = jnp.concatenate([top_face[:, served], top_face[:, served + 1]], axis=0)
        arrived = lax.all_to_all(pairs, "blk", split_axis=1, concat_axis=1, tiled=True)
        first = arrived[:fields][:, slot_index]
        second = arrived[fields:][:, slot_index]
        lower = intersection_weight[None, :] * first + (1.0 - intersection_weight[None, :]) * second
        bottom_face = state[:, 0, :]
        coef = accumulate(
            (
                lax.all_gather(bottom_face[None], "blk", axis=0, tiled=True),
                lax.all_gather(own_terms, "blk", axis=0, tiled=True),
            )
        )
        upper = jnp.einsum("h,hcn->cn", own_basis, coef, precision=lax.Precision.HIGHEST)
        state = update(state, time_source, lower, upper, viscosity, advection, coupling)
    return state


def solution(mesh):
    return jax.shard_map(
        per_device,
        mesh=mesh,
        in_specs=(
            P(None, None, ("groups", "blk")),
            P(None, None, ("groups", "blk")),
            P(None, ("groups", "blk")),
            P(),
            P(),
            P(("groups", "blk"), None),
            P(("groups", "blk")),
            P(("groups", "blk")),
            P(("groups", "blk")),
        ),
        out_specs=P(None, None, ("groups", "blk")),
        check_vma=False,
    )
```

profile of v0, /device:TPU:0, one launch (start us, length us, event | category | flops | bytes accessed | tf_op | source)
XLA Modules:
  0.0 210.1 jit_solution(16810164765573629967)
XLA Ops:
  0.0 0.8 fusion.49
  0.8 1.1 reduce-window.6
  2.2 0.8 fusion.48
  3.6 2.6 %scatter_custom_fusion = s32[1024]{0:T(1024)S(1)} fusion(s32[512]{0:T(512)S(1)} %bitcast.240, s32[512]{0:T(512)} %param.15, s32[]{:T(128)} %constant.8.clone.1), kind=kCustom, calls=%fused_computation.129 | custom fusion | bytes 4608 | tf_op jit(solution)/shard_map/scatter | solution.py:72
  6.9 7.4 %all-to-all-start = ((s32[16,64,1]{1,2,0:T(1,128)}), s32[16,64,1]{1,2,0:T(1,128)S(1)}, u32[]{:S(2)}, u32[]{:S(2)}) async-start(s32[16,64,1]{1,2,0:T(1,128)} %bitcast.6), calls=%async_computation | async-start | bytes 16384 | tf_op jit(solution)/shard_map/all_to_all | solution.py:73
  15.1 21.6 %all-gather.4 = f32[16,1,17]{2,1,0:T(1,128)S(1)} all-gather(f32[1,1,17]{2,1,0:T(1,128)S(1)} %multiply_bitcast_fusion), channel_id=1, replica_groups=mesh['groups'=2,'blk'=16] {'blk'}, dimensions={0}, use_global_device_ids=true | all-gather | bytes 1156 | tf_op jit(solution)/shard_map/all_gather | solution.py:88
  36.7 0.9 fusion.76
  37.7 17.8 %all-gather = f32[80,1,512]{2,1,0:T(1,128)S(1)} all-gather(f32[5,1,512]{2,1,0:T(1,128)S(1)} %get-tuple-element.12), channel_id=2, replica_groups=mesh['groups'=2,'blk'=16] {'blk'}, dimensions={0}, use_global_device_ids=true | all-gather | bytes 174080 | tf_op jit(solution)/shard_map/all_gather | solution.py:87
  58.6 2.8 %gather_fusion.1 = f32[1024,5]{1,0:T(8,128)S(1)} fusion(f32[5,512]{0,1:T(8,128)S(1)} %bitcast.202, s32[1024]{0:T(1024)S(1)} %broadcast_clamp_fusion), kind=kCustom, calls=%fused_computation.1 | custom fusion | bytes 45056 | tf_op jit(solution)/shard_map/gather | solution.py:79
  61.6 2.8 %gather_fusion = f32[1024,5]{1,0:T(8,128)S(1)} fusion(f32[5,512]{0,1:T(8,128)S(1)} %bitcast.203, s32[1024]{0:T(1024)S(1)} %broadcast_clamp_fusion.1), kind=kCustom, calls=%fused_computation | custom fusion | bytes 45056 | tf_op jit(solution)/shard_map/gather | solution.py:79
  64.8 0.7 reshape.533
  65.5 3.5 %all-to-all-start.1 = ((f32[16,1,640]{2,1,0:T(1,128)}), f32[16,1,640]{2,1,0:T(1,128)S(1)}, u32[]{:S(2)}, u32[]{:S(2)}) async-start(f32[16,1,640]{2,1,0:T(1,128)} %reshape.533), calls=%async_computation.1 | async-start | bytes 81920 | tf_op jit(solution)/shard_map/all_to_all | solution.py:80
  69.0 6.6 %all-to-all-done.1 = f32[16,1,640]{2,1,0:T(1,128)S(1)} async-done(((f32[16,1,640]{2,1,0:T(1,128)}), f32[16,1,640]{2,1,0:T(1,128)S(1)}, u32[]{:S(2)}, u32[]{:S(2)}) %all-to-all-start.1) | async-done | bytes 40992 | tf_op jit(solution)/shard_map/all_to_all | solution.py:80
  76.3 0.8 reduce.10
  77.4 1.0 gather_fusion.2
  78.9 1.0 gather_fusion.3
  80.1 2.0 fusion.14
  82.2 2.8 %gather_fusion.5 = f32[1024,5]{1,0:T(8,128)S(1)} fusion(f32[5,512]{0,1:T(8,128)S(1)} %copy.141, s32[1024]{0:T(1024)S(1)} %broadcast_clamp_fusion), kind=kCustom, calls=%fused_computation.5 | custom fusion | bytes 45056 | tf_op jit(solution)/shard_map/gather | solution.py:79
  85.0 2.8 %gather_fusion.4 = f32[1024,5]{1,0:T(8,128)S(1)} fusion(f32[5,512]{0,1:T(8,128)S(1)} %copy.141, s32[1024]{0:T(1024)S(1)} %broadcast_clamp_fusion.1), kind=kCustom, calls=%fused_computation.4 | custom fusion | bytes 45056 | tf_op jit(solution)/shard_map/gather | solution.py:79
  87.9 18.0 %all-gather.1 = f32[80,1,512]{2,1,0:T(1,128)S(1)} all-gather(f32[5,1,512]{2,1,0:T(1,128)S(1)} %copy.150), channel_id=3, replica_groups=mesh['groups'=2,'blk'=16] {'blk'}, dimensions={0}, use_global_device_ids=true | all-gather | bytes 174080 | tf_op jit(solution)/shard_map/all_gather | solution.py:87
  107.2 0.7 reshape.535
  108.0 3.7 %all-to-all-start.2 = ((f32[16,1,640]{2,1,0:T(1,128)}), f32[16,1,640]{2,1,0:T(1,128)S(1)}, u32[]{:S(2)}, u32[]{:S(2)}) async-start(f32[16,1,640]{2,1,0:T(1,128)} %reshape.535), calls=%async_computation.2 | async-start | bytes 81920 | tf_op jit(solution)/shard_map/all_to_all | solution.py:80
  112.0 6.2 %all-to-all-done.2 = f32[16,1,640]{2,1,0:T(1,128)S(1)} async-done(((f32[16,1,640]{2,1,0:T(1,128)}), f32[16,1,640]{2,1,0:T(1,128)S(1)}, u32[]{:S(2)}, u32[]{:S(2)}) %all-to-all-start.2) | async-done | bytes 40992 | tf_op jit(solution)/shard_map/all_to_all | solution.py:80
  118.1 0.8 reduce.11
  119.3 1.0 gather_fusion.6
  120.7 1.0 gather_fusion.7
  121.9 3.1 %fusion.11 = f32[5,64,512]{2,0,1:T(8,128)S(1)} fusion(f32[5,64,512]{2,0,1:T(8,128)S(1)} %fusion.14, f32[5,64,512]{2,1,0:T(8,128)} %param.10, f32[5,1,512]{2,0,1:T(8,128)S(1)} %bitcast.238, f32[5,1,512]{2,0,1:T(8,128)S(1)} %fusion.52, f32[64,512]{1,0:T(8,128)S(1)} %copy-done.6, f32[5]{0:T(128)S(1)} %copy-done.7, f32[5,5]{1,0:T(8,128)S(1)} %copy-done), kind=kOutput, calls=%fused_computation.35 | convolution fusion | flops 12615680 | bytes 3576320 | tf_op jit(solution)/shard_map/cd,djn->cjn/dot_general | solution.py:23
  125.2 2.8 %gather_fusion.9 = f32[1024,5]{1,0:T(8,128)S(1)} fusion(f32[5,512]{0,1:T(8,128)S(1)} %copy.153, s32[1024]{0:T(1024)S(1)} %broadcast_clamp_fusion), kind=kCustom, calls=%fused_computation.9 | custom fusion | bytes 45056 | tf_op jit(solution)/shard_map/gather | solution.py:79
  128.0 2.8 %gather_fusion.8 = f32[1024,5]{1,0:T(8,128)S(1)} fusion(f32[5,512]{0,1:T(8,128)S(1)} %copy.153, s32[1024]{0:T(1024)S(1)} %broadcast_clamp_fusion.1), kind=kCustom, calls=%fused_computation.8 | custom fusion | bytes 45056 | tf_op jit(solution)/shard_map/gather | solution.py:79
  130.8 18.0 %all-gather.2 = f32[80,1,512]{2,1,0:T(1,128)S(1)} all-gather(f32[5,1,512]{2,1,0:T(1,128)S(1)} %copy.162), channel_id=4, replica_groups=mesh['groups'=2,'blk'=16] {'blk'}, dimensions={0}, use_global_device_ids=true | all-gather | bytes 174080 | tf_op jit(solution)/shard_map/all_gather | solution.py:87
  150.2 0.7 reshape.537
  150.9 3.5 %all-to-all-start.3 = ((f32[16,1,640]{2,1,0:T(1,128)}), f32[16,1,640]{2,1,0:T(1,128)S(1)}, u32[]{:S(2)}, u32[]{:S(2)}) async-start(f32[16,1,640]{2,1,0:T(1,128)} %reshape.537), calls=%async_computation.3 | async-start | bytes 81920 | tf_op jit(solution)/shard_map/all_to_all | solution.py:80
  154.8 6.3 %all-to-all-done.3 = f32[16,1,640]{2,1,0:T(1,128)S(1)} async-done(((f32[16,1,640]{2,1,0:T(1,128)}), f32[16,1,640]{2,1,0:T(1,128)S(1)}, u32[]{:S(2)}, u32[]{:S(2)}) %all-to-all-start.3) | async-done | bytes 40992 | tf_op jit(solution)/shard_map/all_to_all | solution.py:80
  161.1 0.8 reduce.12
  162.3 1.0 gather_fusion.10
  163.7 1.0 gather_fusion.11
  164.9 2.1 %fusion.7 = f32[5,64,512]{2,0,1:T(8,128)S(1)} fusion(f32[5,64,512]{2,0,1:T(8,128)S(1)} %fusion.11, f32[5,64,512]{2,1,0:T(8,128)S(1)} %copy-done.4, f32[5,1,512]{2,0,1:T(8,128)S(1)} %bitcast.239, f32[5,1,512]{2,0,1:T(8,128)S(1)} %fusion.51, f32[64,512]{1,0:T(8,128)S(1)} %copy-done.6, f32[5]{0:T(128)S(1)} %copy-done.7, f32[5,5]{1,0:T(8,128)S(1)} %copy-done), kind=kOutput, calls=%fused_computation.30 | convolution fusion | flops 12615680 | bytes 3576320 | tf_op jit(solution)/shard_map/cd,djn->cjn/dot_general | solution.py:23
  167.1 2.8 %gather_fusion.13 = f32[1024,5]{1,0:T(8,128)S(1)} fusion(f32[5,512]{0,1:T(8,128)S(1)} %copy.165, s32[1024]{0:T(1024)S(1)} %broadcast_clamp_fusion), kind=kCustom, calls=%fused_computation.13 | custom fusion | bytes 45056 | tf_op jit(solution)/shard_map/gather | solution.py:79
  170.0 2.8 %gather_fusion.12 = f32[1024,5]{1,0:T(8,128)S(1)} fusion(f32[5,512]{0,1:T(8,128)S(1)} %copy.165, s32[1024]{0:T(1024)S(1)} %broadcast_clamp_fusion.1), kind=kCustom, calls=%fused_computation.12 | custom fusion | bytes 45056 | tf_op jit(solution)/shard_map/gather | solution.py:79
  172.8 18.0 %all-gather.3 = f32[80,1,512]{2,1,0:T(1,128)S(1)} all-gather(f32[5,1,512]{2,1,0:T(1,128)S(1)} %copy.174), channel_id=5, replica_groups=mesh['groups'=2,'blk'=16] {'blk'}, dimensions={0}, use_global_device_ids=true | all-gather | bytes 174080 | tf_op jit(solution)/shard_map/all_gather | solution.py:87
  192.2 0.7 reshape.539
  192.9 3.7 %all-to-all-start.4 = ((f32[16,1,640]{2,1,0:T(1,128)}), f32[16,1,640]{2,1,0:T(1,128)S(1)}, u32[]{:S(2)}, u32[]{:S(2)}) async-start(f32[16,1,640]{2,1,0:T(1,128)} %reshape.539), calls=%async_computation.4 | async-start | bytes 81920 | tf_op jit(solution)/shard_map/all_to_all | solution.py:80
  197.0 6.1 %all-to-all-done.4 = f32[16,1,640]{2,1,0:T(1,128)S(1)} async-done(((f32[16,1,640]{2,1,0:T(1,128)}), f32[16,1,640]{2,1,0:T(1,128)S(1)}, u32[]{:S(2)}, u32[]{:S(2)}) %all-to-all-start.4) | async-done | bytes 40992 | tf_op jit(solution)/shard_map/all_to_all | solution.py:80
  203.1 0.8 reduce.13
  204.2 1.0 gather_fusion.14
  205.6 1.0 gather_fusion.15
  206.8 2.1 fusion.3
  208.9 1.2 copy.176
  (113 shorter events, 14.5 us)
Async XLA Ops:
  0.0 80.0 %copy-start = (f32[5,5]{1,0:T(8,128)S(1)}, f32[5,5]{1,0:T(8,128)}, u32[]{:S(2)}) copy-start(f32[5,5]{1,0:T(8,128)} %param.13) | copy-start | bytes 304
  0.0 56.7 %copy-start.1 = (f32[5,64,512]{2,1,0:T(8,128)S(1)}, f32[5,64,512]{2,1,0:T(8,128)}, u32[]{:S(2)}) copy-start(f32[5,64,512]{2,1,0:T(8,128)} %param.9) | copy-start | bytes 1966084
  0.0 56.7 %copy-start.2 = (f32[512]{0:T(512)S(1)}, f32[512]{0:T(512)}, u32[]{:S(2)}) copy-start(f32[512]{0:T(512)} %param.16) | copy-start | bytes 6148
  6.9 50.4 %all-to-all-start = ((s32[16,64,1]{1,2,0:T(1,128)}), s32[16,64,1]{1,2,0:T(1,128)S(1)}, u32[]{:S(2)}, u32[]{:S(2)}) async-start(s32[16,64,1]{1,2,0:T(1,128)} %bitcast.6), calls=%async_computation | async-start | bytes 16384 | tf_op jit(solution)/shard_map/all_to_all | solution.py:73
  65.5 10.2 %all-to-all-start.1 = ((f32[16,1,640]{2,1,0:T(1,128)}), f32[16,1,640]{2,1,0:T(1,128)S(1)}, u32[]{:S(2)}, u32[]{:S(2)}) async-start(f32[16,1,640]{2,1,0:T(1,128)} %reshape.533), calls=%async_computation.1 | async-start | bytes 81920 | tf_op jit(solution)/shard_map/all_to_all | solution.py:80
  77.2 2.9 %copy-start.3 = (f32[5,64,512]{2,1,0:T(8,128)S(1)}, f32[5,64,512]{2,1,0:T(8,128)}, u32[]{:S(2)}) copy-start(f32[5,64,512]{2,1,0:T(8,128)} %param.10) | copy-start | bytes 1966084
  77.2 2.9 %copy-start.6 = (f32[64,512]{1,0:T(8,128)S(1)}, f32[64,512]{1,0:T(8,128)}, u32[]{:S(2)}) copy-start(f32[64,512]{1,0:T(8,128)} %param.11) | copy-start | bytes 393220
  77.2 2.9 %copy-start.7 = (f32[5]{0:T(128)S(1)}, f32[5]{0:T(128)}, u32[]{:S(2)}) copy-start(f32[5]{0:T(128)} %param.12) | copy-start | bytes 64
  108.0 10.2 %all-to-all-start.2 = ((f32[16,1,640]{2,1,0:T(1,128)}), f32[16,1,640]{2,1,0:T(1,128)S(1)}, u32[]{:S(2)}, u32[]{:S(2)}) async-start(f32[16,1,640]{2,1,0:T(1,128)} %reshape.535), calls=%async_computation.2 | async-start | bytes 81920 | tf_op jit(solution)/shard_map/all_to_all | solution.py:80
  150.9 10.2 %all-to-all-start.3 = ((f32[16,1,640]{2,1,0:T(1,128)}), f32[16,1,640]{2,1,0:T(1,128)S(1)}, u32[]{:S(2)}, u32[]{:S(2)}) async-start(f32[16,1,640]{2,1,0:T(1,128)} %reshape.537), calls=%async_computation.3 | async-start | bytes 81920 | tf_op jit(solution)/shard_map/all_to_all | solution.py:80
  162.0 2.8 %copy-start.4 = (f32[5,64,512]{2,1,0:T(8,128)S(1)}, f32[5,64,512]{2,1,0:T(8,128)}, u32[]{:S(2)}) copy-start(f32[5,64,512]{2,1,0:T(8,128)} %param.10) | copy-start | bytes 1966084
  192.9 10.2 %all-to-all-start.4 = ((f32[16,1,640]{2,1,0:T(1,128)}), f32[16,1,640]{2,1,0:T(1,128)S(1)}, u32[]{:S(2)}, u32[]{:S(2)}) async-start(f32[16,1,640]{2,1,0:T(1,128)} %reshape.539), calls=%async_computation.4 | async-start | bytes 81920 | tf_op jit(solution)/shard_map/all_to_all | solution.py:80
  204.0 2.8 %copy-start.5 = (f32[5,64,512]{2,1,0:T(8,128)S(1)}, f32[5,64,512]{2,1,0:T(8,128)}, u32[]{:S(2)}) copy-start(f32[5,64,512]{2,1,0:T(8,128)} %param.10) | copy-start | bytes 1966084
where the time goes:
time: 211 us; the launch traced here: 210 us
  blocking collectives  93.5 us (44%)
  local copies, waits for them, and re-layouts  46.9 us (22%)
  waiting for transfers between devices  25.3 us (12%)
  starting transfers between devices  21.8 us (10%)
  matrix products  12.1 us (6%)
  other arithmetic  9.09 us (4%)
    all_gather x4, blocking collectives, per_device(): lax.all_gather(bottom_face[None], 'blk', axis=0, tiled=True)  71.9 us
    all_to_all x4, waiting for transfers between devices, per_device(): lax.all_to_all(pairs, 'blk', split_axis=1, concat_axis=1, tiled=True)  25.3 us
    all_gather x1, blocking collectives, per_device(): lax.all_gather(own_terms, 'blk', axis=0, tiled=True)  21.6 us
    all_to_all x4, starting transfers between devices, per_device(): lax.all_to_all(pairs, 'blk', split_axis=1, concat_axis=1, tiled=True)  14.4 us
    gather x8, local copies, waits for them, and re-layouts, per_device(): top_face[:, served]  12.1 us
    gather x8, local copies, waits for them, and re-layouts, per_device(): top_face[:, served + 1]  12 us
    dot_general x4, matrix products, stencil(): jnp.einsum('cd,djn->cjn', coupling, block, precision=lax.Precision.HIGHEST)  9.29 us
    all_to_all x1, starting transfers between devices, per_device(): lax.all_to_all(wanted, 'blk', split_axis=0, concat_axis=0, tiled=True)  7.39 us
  transfers between devices with their start and end apart: 5, of which 4 were waited for; matrix products, arithmetic and copies ran while one was open for 2% of the time, Pallas kernels for 0%

commit v1 on v0

v1 whole, which is shorter than its diff:
```python
import functools
import math

import jax
import jax.numpy as jnp
from jax import lax
from jax.experimental import pallas as pl
from jax.experimental.pallas import tpu as pltpu
from jax.sharding import PartitionSpec as P

HARM = 8
PHASES = 512
LAG = 37
ITERS = 4
PSEUDO = 0.2
LANES = 128
SUB = 8
EXACT = lax.Precision.HIGHEST


class Sizes:
    def __init__(self, fields, rows, width, blocks):
        self.fields, self.rows, self.width, self.blocks = fields, rows, width, blocks
        self.groups = width // LANES
        self.cap = 2 * width // blocks
        self.packs = LANES // self.cap
        self.tops = 0
        self.bottoms = self.tops + ITERS * fields * self.groups
        self.visc = self.bottoms + ITERS * fields * self.groups
        self.slot = self.visc + 4 * self.groups
        self.offsets = self.slot + self.groups
        self.weights = self.offsets + SUB
        self.terms = self.weights + SUB
        self.basis = self.terms + 1
        self.table = -(-(self.basis + 1) // SUB) * SUB


def matrix_of(sz, advection, coupling):
    own = [[-PSEUDO * coupling[c, d] for d in range(sz.fields)] for c in range(sz.fields)]
    speed = [PSEUDO * advection[c] for c in range(sz.fields)]
    for c in range(sz.fields):
        own[c][c] = own[c][c] + ((1.0 - 1.5 * PSEUDO) - speed[c])
    return own, speed


def shifted_west(u):
    lane = lax.broadcasted_iota(jnp.int32, u.shape, 1)
    return jnp.where(lane == 0, 0.0, pltpu.roll(u, 1, axis=1))


def shifted_east(u):
    width = u.shape[1]
    lane = lax.broadcasted_iota(jnp.int32, u.shape, 1)
    return jnp.where(lane == width - 1, 0.0, pltpu.roll(u, width - 1, axis=1))


def advance(sz, own, speed, u, visc, column, source):
    out = []
    for c in range(sz.fields):
        west, east = shifted_west(u[c]), shifted_east(u[c])
        new = speed[c] * west + visc * (west + east + column(c) - 4.0 * u[c])
        for d in range(sz.fields):
            new = new + own[c][d] * u[d]
        if source is not None:
            new = new - source(c)
        out.append(new)
    return out


def edge_column(u, ghost, at_low):
    row = lax.broadcasted_iota(jnp.int32, u.shape, 0)
    up, down = pltpu.roll(u, 1, axis=0), pltpu.roll(u, SUB - 1, axis=0)
    if at_low:
        return jnp.where(row == 0, ghost, up) + down
    return up + jnp.where(row == SUB - 1, ghost, down)


def prepare_kernel(
    sz, adv_ref, coup_ref, phase_ref, low_u, high_u, low_q, high_q, low_v, high_v, owner_ref, offset_ref, weight_ref, out_ref
):
    own, speed = matrix_of(sz, adv_ref, coup_ref)

    def put(at, row):
        for g in range(sz.groups):
            out_ref[at + g : at + g + 1, :] = row[:, g * LANES : (g + 1) * LANES]

    out_ref[sz.basis : sz.table, :] = jnp.zeros((sz.table - sz.basis, LANES), jnp.float32)
    for side, (u_ref, q_ref, v_ref, at_low) in enumerate(
        ((high_u, high_q, high_v, False), (low_u, low_q, low_v, True))
    ):
        face = 0 if at_low else SUB - 1
        inner = 1 if at_low else SUB - 2
        base = sz.bottoms if at_low else sz.tops
        visc = PSEUDO * v_ref[...]
        put(sz.visc + (2 * side) * sz.groups, visc[face : face + 1])
        put(sz.visc + (2 * side + 1) * sz.groups, visc[inner : inner + 1])
        u = [u_ref[c] for c in range(sz.fields)]
        q = [PSEUDO * q_ref[c] for c in range(sz.fields)]
        for k in range(ITERS):
            for c in range(sz.fields):
                put(base + (k * sz.fields + c) * sz.groups, u[c][face : face + 1])
            if k < ITERS - 1:
                u = advance(sz, own, speed, u, visc, lambda c: edge_column(u[c], 0.0, at_low), lambda c: q[c])

    owner, offset, weight = owner_ref[...], offset_ref[...], weight_ref[...]
    member = lax.broadcasted_iota(jnp.int32, (sz.blocks, sz.width), 0) == owner
    member = member.astype(jnp.bfloat16)
    before = lax.broadcasted_iota(jnp.int32, (sz.width, sz.width), 0) <= lax.broadcasted_iota(
        jnp.int32, (sz.width, sz.width), 1
    )
    count = jnp.dot(member, before.astype(jnp.bfloat16), preferred_element_type=jnp.float32)
    rank = jnp.sum(count * member.astype(jnp.float32), axis=0, keepdims=True) - 1.0
    rank = rank.astype(jnp.int32)
    slot = owner * sz.cap + rank
    put(sz.slot, slot.astype(jnp.float32))
    place = (lax.broadcasted_iota(jnp.int32, (LANES, sz.width), 0) == slot % LANES).astype(jnp.float32)
    held = lax.broadcasted_iota(jnp.int32, (SUB, sz.width), 0) == slot // LANES
    values = jnp.concatenate(
        [jnp.where(held, offset.astype(jnp.float32), 0.0), jnp.where(held, weight, 0.0)], axis=0
    )
    tables = lax.dot_general(
        values, place, (((1,), (1,)), ((), ())), precision=EXACT, preferred_element_type=jnp.float32
    )
    out_ref[sz.offsets : sz.offsets + 2 * SUB, :] = tables

    order = lax.broadcasted_iota(jnp.int32, (1, LANES), 1)
    harmonic = jnp.where(order > HARM, order - HARM, order).astype(jnp.float32)
    used = order <= 2 * HARM

    def waves(angle):
        product = angle * harmonic
        return jnp.where(order <= HARM, jnp.cos(product), jnp.sin(product))

    phase = phase_ref[0].astype(jnp.float32)
    scale = jnp.where(order == 0, 1.0, 2.0) / sz.blocks
    terms = waves(phase * (2.0 * math.pi / PHASES)) * scale
    basis = waves((phase + LAG) * (2.0 * math.pi / PHASES))
    out_ref[sz.terms : sz.terms + 1, :] = jnp.where(used, terms, 0.0)
    out_ref[sz.basis : sz.basis + 1, :] = jnp.where(used, basis, 0.0)


def interior_kernel(sz, adv_ref, coup_ref, u_ref, q_ref, v_ref, out_ref, work):
    own, speed = matrix_of(sz, adv_ref, coup_ref)
    tiles = sz.rows // SUB
    row = lax.broadcasted_iota(jnp.int32, (SUB, sz.width), 0)
    for k in range(ITERS):
        src = u_ref if k == 0 else work.at[(k - 1) % 2]
        dst = out_ref if k == ITERS - 1 else work.at[k % 2]
        for t in range(tiles):
            here = slice(t * SUB, (t + 1) * SUB)
            u = [src[c, here, :] for c in range(sz.fields)]

            def column(c):
                up, down = pltpu.roll(u[c], 1, axis=0), pltpu.roll(u[c], SUB - 1, axis=0)
                above = src[c, t * SUB - 1 : t * SUB, :] if t > 0 else 0.0
                below = src[c, (t + 1) * SUB : (t + 1) * SUB + 1, :] if t < tiles - 1 else 0.0
                return jnp.where(row == 0, above, up) + jnp.where(row == SUB - 1, below, down)

            new = advance(sz, own, speed, u, PSEUDO * v_ref[here, :], column, lambda c: PSEUDO * q_ref[c, here, :])
            for c in range(sz.fields):
                dst[c, here, :] = new[c]


def couple_kernel(
    sz,
    adv_ref,
    coup_ref,
    me_ref,
    even_ref,
    odd_ref,
    low_u,
    high_u,
    low_q,
    high_q,
    low_v,
    high_v,
    out_ref,
    slot_offset,
    slot_weight,
    slot_value,
    top_ref,
    next_ref,
    lower_ref,
    bottom_ref,
):
    own, speed = matrix_of(sz, adv_ref, coup_ref)
    me = me_ref[0]
    packs, groups, fields = sz.packs, sz.groups, sz.fields
    stride = packs // 2 * sz.table
    lane = lax.broadcasted_iota(jnp.int32, (SUB, LANES), 1)

    def line(b, row):
        ref = (even_ref, odd_ref)[b % 2]
        return ref[pl.ds(b // 2 * sz.table + row, SUB, stride=stride), :]

    def wide(b, row):
        return jnp.concatenate([line(b, row + g) for g in range(groups)], axis=1)

    for m in range(SUB):
        offsets = [line(b, sz.offsets + m) for b in range(packs)]
        weights = [line(b, sz.weights + m) for b in range(packs)]
        for n in range(packs):
            tile_o, tile_w = offsets[n], weights[n]
            for b in range(packs):
                if b != n:
                    mine = lane // sz.cap == b
                    turn = (b - n) * sz.cap % LANES
                    tile_o = jnp.where(mine, pltpu.roll(offsets[b], turn, axis=1), tile_o)
                    tile_w = jnp.where(mine, pltpu.roll(weights[b], turn, axis=1), tile_w)
            o = jnp.bitwise_xor(m * packs + n, me)
            slot_offset[o] = tile_o.astype(jnp.int32)
            slot_weight[o] = tile_w

    slots = [wide(b, sz.slot).astype(jnp.int32) for b in range(packs)]
    takers = [jnp.bitwise_xor(s // sz.cap, me) for s in slots]
    places = [s % sz.cap + b * sz.cap for b, s in enumerate(slots)]
    basis = jnp.concatenate([line(b, sz.basis) for b in range(packs)], axis=0)
    terms = jnp.concatenate([line(b, sz.terms) for b in range(packs)], axis=0)
    kernel = lax.dot_general(
        basis, terms, (((1,), (1,)), ((), ())), precision=EXACT, preferred_element_type=jnp.float32
    )

    def gather(tiles):
        def first_stage(o, carry):
            offset, weight = slot_offset[o], slot_weight[o]
            at, part = offset % LANES, offset // LANES
            for c in range(fields):
                pair = []
                for ref in (top_ref, next_ref):
                    value = None
                    for g in range(groups):
                        source = jnp.broadcast_to(ref[g, o, c : c + 1, :], (SUB, LANES))
                        taken = jnp.take_along_axis(source, at, axis=1)
                        value = taken if value is None else jnp.where(part == g, taken, value)
                    pair.append(value)
                slot_value[o, c] = weight * pair[0] + (1.0 - weight) * pair[1]
            return carry

        lax.fori_loop(0, sz.blocks, first_stage, 0, unroll=2)
        for b in tiles:
            for g in range(groups):
                cells = slice(g * LANES, (g + 1) * LANES)
                taker, place = takers[b][:, cells], places[b][:, cells]

                def second_stage(o, found):
                    mine = taker == o
                    return tuple(
                        jnp.where(mine, jnp.take_along_axis(slot_value[o, c], place, axis=1), found[c])
                        for c in range(fields)
                    )

                zero = jnp.zeros((SUB, LANES), jnp.float32)
                found = lax.fori_loop(0, sz.blocks, second_stage, (zero,) * fields, unroll=4)
                for c in range(fields):
                    lower_ref[b, c, :, cells] = found[c]

    def face_step(e, visc, extra):
        return advance(sz, own, speed, e, visc, extra, None)

    visc = {}
    for b in range(packs):
        for n, name in enumerate(("top", "top_in", "bottom", "bottom_in")):
            visc[name, b] = wide(b, sz.visc + n * groups)

    blocks = range(packs)
    outer = {}
    inner = {}
    state = {True: [low_u[c] for c in range(fields)], False: [high_u[c] for c in range(fields)]}
    sources = {True: low_q, False: high_q}
    viscs = {True: PSEUDO * low_v[...], False: PSEUDO * high_v[...]}
    for k in range(ITERS):
        for b in blocks:
            for c in range(fields):
                top = wide(b, sz.tops + (k * fields + c) * groups)
                bottom = wide(b, sz.bottoms + (k * fields + c) * groups)
                if k > 0:
                    top, bottom = top + outer["top", b][c], bottom + outer["bottom", b][c]
                rows = pl.ds(b * SUB + c, SUB, stride=packs * SUB)
                after = pltpu.roll(top, sz.width - 1, axis=1)
                for g in range(groups):
                    cells = slice(g * LANES, (g + 1) * LANES)
                    top_ref.reshape(groups, sz.blocks * SUB, LANES)[g, rows, :] = top[:, cells]
                    next_ref.reshape(groups, sz.blocks * SUB, LANES)[g, rows, :] = after[:, cells]
                bottom_ref[c, b * SUB : (b + 1) * SUB, :] = bottom
        gather(blocks if k < ITERS - 1 else blocks[:1])
        upper = [
            jnp.dot(kernel, bottom_ref[c], precision=EXACT, preferred_element_type=jnp.float32) for c in range(fields)
        ]
        if k < ITERS - 1:
            for b in blocks:
                ghosts = {
                    "top": [upper[c][b * SUB : (b + 1) * SUB] for c in range(fields)],
                    "bottom": [lower_ref[b, c] for c in range(fields)],
                }
                for name, ghost in ghosts.items():
                    v, v_in = visc[name, b], visc[name + "_in", b]
                    if k == 0:
                        outer[name, b] = [v * ghost[c] for c in range(fields)]
                    else:
                        e, e_in = outer[name, b], inner.get((name, b))
                        inner[name, b] = [v_in * e[c] for c in range(fields)]
                        outer[name, b] = face_step(
                            e, v, lambda c: ghost[c] if e_in is None else ghost[c] + e_in[c]
                        )
        for at_low in (True, False):
            u, q = state[at_low], sources[at_low]
            ghost = [(lower_ref[0, c] if at_low else upper[c])[0:1] for c in range(fields)]
            state[at_low] = advance(
                sz, own, speed, u, viscs[at_low], lambda c: edge_column(u[c], ghost[c], at_low), lambda c: PSEUDO * q[c]
            )
    for c in range(fields):
        out_ref[0, c] = state[True][c]
        out_ref[1, c] = state[False][c]


def spread(table, blocks):
    parts = [table]
    bit = 2
    while bit < blocks:
        masks = [bit] if bit == 2 or 2 * bit >= blocks else [bit, 2 * bit, 3 * bit]
        have = jnp.concatenate(parts, axis=0)
        parts = [have] + [lax.ppermute(have, "blk", [(i, i ^ m) for i in range(blocks)]) for m in masks]
        bit = bit * (len(masks) + 1)
    even = jnp.concatenate(parts, axis=0)
    odd = lax.ppermute(even, "blk", [(i, i ^ 1) for i in range(blocks)])
    return even, odd


def per_device(
    state_now,
    time_source,
    viscosity,
    advection,
    coupling,
    owner_list,
    owner_offset,
    intersection_weight,
    phase_index,
):
    blocks = lax.axis_size("blk")
    fields, rows, width = state_now.shape
    sz = Sizes(fields, rows, width, blocks)
    me = lax.axis_index("blk").astype(jnp.int32).reshape(1)
    smem = pl.BlockSpec(memory_space=pltpu.SMEM)
    vmem = pl.BlockSpec(memory_space=pltpu.VMEM)
    ends = [
        pl.BlockSpec((fields, SUB, width), lambda i: (0, 0, 0)),
        pl.BlockSpec((fields, SUB, width), lambda i: (0, rows // SUB - 1, 0)),
    ]
    visc_ends = [
        pl.BlockSpec((SUB, width), lambda i: (0, 0)),
        pl.BlockSpec((SUB, width), lambda i: (rows // SUB - 1, 0)),
    ]
    edges = [state_now, state_now, time_source, time_source, viscosity, viscosity]
    line = pl.BlockSpec((1, width), lambda i: (0, 0))
    limit = pltpu.CompilerParams(vmem_limit_bytes=50 * 1024 * 1024)
    table = pl.pallas_call(
        functools.partial(prepare_kernel, sz),
        grid=(1,),
        out_shape=jax.ShapeDtypeStruct((sz.table, LANES), jnp.float32),
        in_specs=[smem, smem, smem] + ends + ends + visc_ends + [line] * 3,
        out_specs=pl.BlockSpec((sz.table, LANES), lambda i: (0, 0)),
        compiler_params=limit,
    )(
        advection,
        coupling,
        phase_index,
        *edges,
        owner_list.reshape(1, width),
        owner_offset.reshape(1, width),
        intersection_weight.reshape(1, width),
    )
    even, odd = spread(table, blocks)
    inside = pl.pallas_call(
        functools.partial(interior_kernel, sz),
        out_shape=jax.ShapeDtypeStruct((fields, rows, width), jnp.float32),
        in_specs=[smem, smem, vmem, vmem, vmem],
        out_specs=vmem,
        scratch_shapes=[pltpu.VMEM((2, fields, rows, width), jnp.float32)],
        compiler_params=limit,
    )(advection, coupling, state_now, time_source, viscosity)
    whole = pl.BlockSpec((blocks // 2 * sz.table, LANES), lambda i: (0, 0))
    strips = pl.pallas_call(
        functools.partial(couple_kernel, sz),
        grid=(1,),
        out_shape=jax.ShapeDtypeStruct((2, fields, SUB, width), jnp.float32),
        in_specs=[smem, smem, smem, whole, whole] + ends + ends + visc_ends,
        out_specs=pl.BlockSpec((2, fields, SUB, width), lambda i: (0, 0, 0, 0)),
        scratch_shapes=[
            pltpu.VMEM((blocks, SUB, LANES), jnp.int32),
            pltpu.VMEM((blocks, SUB, LANES), jnp.float32),
            pltpu.VMEM((blocks, fields, SUB, LANES), jnp.float32),
            pltpu.VMEM((sz.groups, blocks, SUB, LANES), jnp.float32),
            pltpu.VMEM((sz.groups, blocks, SUB, LANES), jnp.float32),
            pltpu.VMEM((sz.packs, fields, SUB, width), jnp.float32),
            pltpu.VMEM((fields, blocks, width), jnp.float32),
        ],
        compiler_params=limit,
    )(advection, coupling, me, even, odd, *edges)
    half = SUB // 2
    return jnp.concatenate([strips[0, :, :half], inside[:, half : rows - half], strips[1, :, half:]], axis=1)


def solution(mesh):
    return jax.shard_map(
        per_device,
        mesh=mesh,
        in_specs=(
            P(None, None, ("groups", "blk")),
            P(None, None, ("groups", "blk")),
            P(None, ("groups", "blk")),
            P(),
            P(),
            P(("groups", "blk"), None),
            P(("groups", "blk")),
            P(("groups", "blk")),
            P(("groups", "blk")),
        ),
        out_specs=P(None, None, ("groups", "blk")),
        check_vma=False,
    )
```

time: 211 us -> 57.5 us (0.27)
  blocking collectives: 93.5 us -> 0 us
  local copies, waits for them, and re-layouts: 46.9 us -> 6.25 us
  Pallas kernels: 0 us -> 23.6 us
  starting transfers between devices: 21.8 us -> 7.63 us
  matrix products: 12.1 us -> 0 us
  other arithmetic: 9.09 us -> 0.95 us
  waiting for transfers between devices: 25.3 us -> 17.6 us
    all_gather x5 -> x0, blocking collectives: 93.5 us -> none  [the longest x4 71.9 us: per_device(): lax.all_gather(bottom_face[None], 'blk', axis=0, tiled=True)]
    gather x32 -> x0, local copies, waits for them, and re-layouts: 33.2 us -> none  [the longest x8 12.1 us: per_device(): top_face[:, served]]
    all_to_all x5 -> x0, waiting for transfers between devices: 25.3 us -> none  [the longest x4 25.3 us: per_device(): lax.all_to_all(pairs, 'blk', split_axis=1, concat_axis=1, tiled=True)]
    pallas_call x0 -> x3, Pallas kernels: none -> 23.6 us  [the longest x1 19.1 us: per_device(): pl.pallas_call(functools.partial(couple_kernel, sz), grid=(1,), out_shape...]
    all_to_all x5 -> x0, starting transfers between devices: 21.8 us -> none  [the longest x4 14.4 us: per_device(): lax.all_to_all(pairs, 'blk', split_axis=1, concat_axis=1, tiled=True)]
    ppermute x0 -> x5, waiting for transfers between devices: none -> 17.6 us  [the longest x4 17.6 us: spread(): lax.ppermute(have, 'blk', [(i, i ^ m) for i in range(blocks)])]
    dot_general x12 -> x0, matrix products: 12.1 us -> none  [the longest x4 9.29 us: stencil(): jnp.einsum('cd,djn->cjn', coupling, block, precision=lax.Precision.HIGHEST)]
    ppermute x0 -> x5, starting transfers between devices: none -> 7.63 us  [the longest x4 7.56 us: spread(): lax.ppermute(have, 'blk', [(i, i ^ m) for i in range(blocks)])]
  transfers between devices with their start and end apart: 5 -> 5, of which waited for: 4 -> 3; matrix products, arithmetic and copies ran while one was open for 2% -> 0% of each run, Pallas kernels for 0% -> 5%
where the time goes in v1:
time: 57.5 us; the launch traced here: 56.8 us
  Pallas kernels  23.6 us (41%)
  waiting for transfers between devices  17.6 us (31%)
  starting transfers between devices  7.63 us (13%)
  local copies, waits for them, and re-layouts  6.25 us (11%)
  other arithmetic  0.95 us (2%)
  between operations  0.81 us (1%)
    pallas_call x1, Pallas kernels, per_device(): pl.pallas_call(functools.partial(couple_kernel, sz), grid=(1,), out_shape...  19.1 us
    ppermute x4, waiting for transfers between devices, spread(): lax.ppermute(have, 'blk', [(i, i ^ m) for i in range(blocks)])  17.6 us
    ppermute x4, starting transfers between devices, spread(): lax.ppermute(have, 'blk', [(i, i ^ m) for i in range(blocks)])  7.56 us
    unnamed x26, local copies, waits for them, and re-layouts  6.15 us
    pallas_call x1, Pallas kernels, per_device(): pl.pallas_call(functools.partial(interior_kernel, sz), out_shape=jax.Shap...  3.1 us
    pallas_call x1, Pallas kernels, per_device(): pl.pallas_call(functools.partial(prepare_kernel, sz), grid=(1,), out_shap...  1.42 us
  transfers between devices with their start and end apart: 5, of which 3 were waited for; matrix products, arithmetic and copies ran while one was open for 0% of the time, Pallas kernels for 5%

profile of v1, /device:TPU:0, one launch (start us, length us, event | category | flops | bytes accessed | tf_op | source)
XLA Modules:
  0.0 56.8 jit_solution(3205099984832518067)
XLA Ops:
  0.0 0.0 copy-start.6
  0.7 0.0 copy-start.8
  0.7 0.0 copy-start.7
  0.7 0.0 copy-done.6
  0.7 0.7 %copy-done.8 = s32[512,1]{0,1:T(1,128)S(1)} copy-done((s32[512,1]{0,1:T(1,128)S(1)}, s32[512,1]{0,1:T(1,128)}, u32[]{:S(2)}) %copy-start.8) | copy-done | bytes 2072
  1.4 0.0 copy-done.7
  1.4 0.0 copy-start
  1.4 1.1 %copy-done = f32[5,64,512]{2,1,0:T(8,128)S(1)} copy-done((f32[5,64,512]{2,1,0:T(8,128)S(1)}, f32[5,64,512]{2,1,0:T(8,128)}, u32[]{:S(2)}) %copy-start) | copy-done | bytes 655384
  2.4 0.0 copy-start.2
  2.4 1.1 %copy-done.2 = f32[5,64,512]{2,1,0:T(8,128)S(1)} copy-done((f32[5,64,512]{2,1,0:T(8,128)S(1)}, f32[5,64,512]{2,1,0:T(8,128)}, u32[]{:S(2)}) %copy-start.2) | copy-done | bytes 655384
  3.5 0.0 copy-start.4
  3.5 0.9 %copy-done.4 = f32[64,512]{1,0:T(8,128)S(1)} copy-done((f32[64,512]{1,0:T(8,128)S(1)}, f32[64,512]{1,0:T(8,128)}, u32[]{:S(2)}) %copy-start.4) | copy-done | bytes 131096
  4.4 0.0 copy-start.9
  4.4 0.7 %copy-done.9 = s32[512]{0:T(512)S(1)} copy-done((s32[512]{0:T(512)S(1)}, s32[512]{0:T(512)}, u32[]{:S(2)}) %copy-start.9) | copy-done | bytes 2072
  5.1 0.0 copy-start.10
  5.1 0.7 %copy-done.10 = f32[512]{0:T(512)S(1)} copy-done((f32[512]{0:T(512)S(1)}, f32[512]{0:T(512)}, u32[]{:S(2)}) %copy-start.10) | copy-done | bytes 2072
  5.8 1.4 %shard_map.91 = f32[200,128]{1,0:T(8,128)S(1)} custom-call(f32[5]{0:T(128)S(1)} %copy-done.7, f32[5,5]{1,0:T(8,128)S(1)} %copy-done.6, s32[1]{0:T(128)S(6)} %copy.14.phase_ref, f32[5,64,512]{2,1,0:T(8,128)S(1)} %copy-done, f32[5,64,512]{2,1,0:T(8,128)S(1)} %copy-done, f32[5,64,512]{2,1,0:T(8,128)S(1)} %copy-done.2, f32[5,64,512]{2,1,0:T(8,128)S(1)} %copy-done.2, ...), custom_call_target="tpu_custom_call" | custom-call | tf_op jit(solution)/shard_map/pallas_call | solution.py:357
  7.2 3.0 %collective-permute-start = (f32[200,128]{1,0:T(8,128)S(1)}, f32[200,128]{1,0:T(8,128)S(1)}, u32[]{:S(2)}, u32[]{:S(2)}) collective-permute-start(f32[200,128]{1,0:T(8,128)S(1)} %shard_map.91), channel_id=1, source_target_pairs={{0,2},{1,3},{2,0},{3,1},{4,6},{5,7},{6,4},{7,5},{8,10},{9,11},{10,... | collective-permute-start | bytes 307208 | tf_op jit(solution)/shard_map/ppermute | solution.py:322
  10.2 2.9 %collective-permute-done = f32[200,128]{1,0:T(8,128)S(1)} collective-permute-done((f32[200,128]{1,0:T(8,128)S(1)}, f32[200,128]{1,0:T(8,128)S(1)}, u32[]{:S(2)}, u32[]{:S(2)}) %collective-permute-start) | collective-permute-done | bytes 102432 | tf_op jit(solution)/shard_map/ppermute | solution.py:322
  13.1 1.9 %collective-permute-start.1 = (f32[400,128]{1,0:T(8,128)S(1)}, f32[400,128]{1,0:T(8,128)S(1)}, u32[]{:S(2)}, u32[]{:S(2)}) collective-permute-start(f32[400,128]{1,0:T(8,128)S(1)} %pad_maximum_fusion.1), channel_id=1, source_target_pairs={{0,4},{1,5},{2,6},{3,7},{4,0},{5,1},{6,2},{7,3},{8,12},{9,13},{10,... | collective-permute-start | bytes 614408 | tf_op jit(solution)/shard_map/ppermute | solution.py:322
  15.0 2.7 %collective-permute-start.2 = (f32[400,128]{1,0:T(8,128)S(1)}, f32[400,128]{1,0:T(8,128)S(1)}, u32[]{:S(2)}, u32[]{:S(2)}) collective-permute-start(f32[400,128]{1,0:T(8,128)S(1)} %pad_maximum_fusion.1), channel_id=1, source_target_pairs={{0,8},{1,9},{2,10},{3,11},{4,12},{5,13},{6,14},{7,15},{8,0},{9,1},... | collective-permute-start | bytes 614408 | tf_op jit(solution)/shard_map/ppermute | solution.py:322
  17.7 0.0 collective-permute-start.3
  17.7 4.6 %collective-permute-done.1 = f32[400,128]{1,0:T(8,128)S(1)} collective-permute-done((f32[400,128]{1,0:T(8,128)S(1)}, f32[400,128]{1,0:T(8,128)S(1)}, u32[]{:S(2)}, u32[]{:S(2)}) %collective-permute-start.1) | collective-permute-done | bytes 204832 | tf_op jit(solution)/shard_map/ppermute | solution.py:322
  22.3 10.1 %collective-permute-done.2 = f32[400,128]{1,0:T(8,128)S(1)} collective-permute-done((f32[400,128]{1,0:T(8,128)S(1)}, f32[400,128]{1,0:T(8,128)S(1)}, u32[]{:S(2)}, u32[]{:S(2)}) %collective-permute-start.2) | collective-permute-done | bytes 204832 | tf_op jit(solution)/shard_map/ppermute | solution.py:322
  32.4 0.0 collective-permute-done.3
  32.5 0.1 collective-permute-start.4
  32.5 0.0 copy-start.3
  32.5 3.1 %shard_map.93 = f32[5,64,512]{2,1,0:T(8,128)S(1)} custom-call(f32[5]{0:T(128)S(1)} %copy-done.7, f32[5,5]{1,0:T(8,128)S(1)} %copy-done.6, f32[5,64,512]{2,1,0:T(8,128)S(1)} %copy-done, f32[5,64,512]{2,1,0:T(8,128)S(1)} %copy-done.2, f32[64,512]{1,0:T(8,128)S(1)} %copy-done.4), custom_call_target="tpu_custom_call" | custom-call | tf_op jit(solution)/shard_map/pallas_call | solution.py:374
  35.7 0.0 copy-start.1
  35.7 0.0 copy-start.5
  35.7 0.1 slice.13
  35.7 0.0 collective-permute-done.4.odd_ref
  35.8 0.0 copy-done.3
  35.8 1.0 %copy-done.1 = f32[5,64,512]{2,1,0:T(8,128)S(1)} copy-done((f32[5,64,512]{2,1,0:T(8,128)S(1)}, f32[5,64,512]{2,1,0:T(8,128)}, u32[]{:S(2)}) %copy-start.1) | copy-done | bytes 655384
  36.7 0.0 copy-done.5
  36.8 19.1 %shard_map.92 = f32[2,5,8,512]{3,2,1,0:T(8,128)S(1)} custom-call(f32[5]{0:T(128)S(1)} %copy-done.7, f32[5,5]{1,0:T(8,128)S(1)} %copy-done.6, s32[1]{0:T(128)} %bitcast.me_ref, f32[1600,128]{1,0:T(8,128)S(1)} %constant_dynamic-update-slice_fusion.even_ref, f32[1600,128]{1,0:T(8,128)} %collective-permute-done.4.odd_ref, f32[5,64,512]{2,1,0:T(8,128)S(1)} %copy-done.1, ...), custom_call_target="tpu_custom_call" | custom-call | tf_op jit(solution)/shard_map/pallas_call | solution.py:383
  55.9 0.9 %pad_maximum_fusion = f32[5,64,512]{2,1,0:T(8,128)} fusion(f32[5,4,512]{2,1,0:T(4,128)S(1)} %get-tuple-element.6, f32[5,56,512]{2,1,0:T(8,128)S(1)} %slice.13, f32[5,4,512]{2,1,0:T(4,128)S(1)} %get-tuple-element.5), kind=kLoop, calls=%fused_computation | loop fusion | flops 327680 | bytes 1310720 | tf_op jit(solution)/shard_map/concatenate | solution.py:401
  (7 shorter events, 0.1 us)
Async XLA Ops:
  0.0 0.7 %copy-start.6 = (f32[5,5]{1,0:T(8,128)S(1)}, f32[5,5]{1,0:T(8,128)}, u32[]{:S(2)}) copy-start(f32[5,5]{1,0:T(8,128)} %coup_ref.5) | copy-start | bytes 304
  0.7 0.7 %copy-start.8 = (s32[512,1]{0,1:T(1,128)S(1)}, s32[512,1]{0,1:T(1,128)}, u32[]{:S(2)}) copy-start(s32[512,1]{0,1:T(1,128)} %param.14) | copy-start | bytes 6148
  0.7 0.7 %copy-start.7 = (f32[5]{0:T(128)S(1)}, f32[5]{0:T(128)}, u32[]{:S(2)}) copy-start(f32[5]{0:T(128)} %adv_ref.5) | copy-start | bytes 64
  1.4 1.1 %copy-start = (f32[5,64,512]{2,1,0:T(8,128)S(1)}, f32[5,64,512]{2,1,0:T(8,128)}, u32[]{:S(2)}) copy-start(f32[5,64,512]{2,1,0:T(8,128)} %u_ref.1) | copy-start | bytes 1966084
  2.4 1.1 %copy-start.2 = (f32[5,64,512]{2,1,0:T(8,128)S(1)}, f32[5,64,512]{2,1,0:T(8,128)}, u32[]{:S(2)}) copy-start(f32[5,64,512]{2,1,0:T(8,128)} %q_ref.1) | copy-start | bytes 1966084
  3.5 0.9 %copy-start.4 = (f32[64,512]{1,0:T(8,128)S(1)}, f32[64,512]{1,0:T(8,128)}, u32[]{:S(2)}) copy-start(f32[64,512]{1,0:T(8,128)} %v_ref.1) | copy-start | bytes 393220
  4.4 0.7 %copy-start.9 = (s32[512]{0:T(512)S(1)}, s32[512]{0:T(512)}, u32[]{:S(2)}) copy-start(s32[512]{0:T(512)} %param.15) | copy-start | bytes 6148
  5.1 0.7 %copy-start.10 = (f32[512]{0:T(512)S(1)}, f32[512]{0:T(512)}, u32[]{:S(2)}) copy-start(f32[512]{0:T(512)} %param.16) | copy-start | bytes 6148
  7.2 5.9 %collective-permute-start = (f32[200,128]{1,0:T(8,128)S(1)}, f32[200,128]{1,0:T(8,128)S(1)}, u32[]{:S(2)}, u32[]{:S(2)}) collective-permute-start(f32[200,128]{1,0:T(8,128)S(1)} %shard_map.91), channel_id=1, source_target_pairs={{0,2},{1,3},{2,0},{3,1},{4,6},{5,7},{6,4},{7,5},{8,10},{9,11},{10,... | collective-permute-start | bytes 307208 | tf_op jit(solution)/shard_map/ppermute | solution.py:322
  13.1 9.2 %collective-permute-start.1 = (f32[400,128]{1,0:T(8,128)S(1)}, f32[400,128]{1,0:T(8,128)S(1)}, u32[]{:S(2)}, u32[]{:S(2)}) collective-permute-start(f32[400,128]{1,0:T(8,128)S(1)} %pad_maximum_fusion.1), channel_id=1, source_target_pairs={{0,4},{1,5},{2,6},{3,7},{4,0},{5,1},{6,2},{7,3},{8,12},{9,13},{10,... | collective-permute-start | bytes 614408 | tf_op jit(solution)/shard_map/ppermute | solution.py:322
  15.0 17.4 %collective-permute-start.2 = (f32[400,128]{1,0:T(8,128)S(1)}, f32[400,128]{1,0:T(8,128)S(1)}, u32[]{:S(2)}, u32[]{:S(2)}) collective-permute-start(f32[400,128]{1,0:T(8,128)S(1)} %pad_maximum_fusion.1), channel_id=1, source_target_pairs={{0,8},{1,9},{2,10},{3,11},{4,12},{5,13},{6,14},{7,15},{8,0},{9,1},... | collective-permute-start | bytes 614408 | tf_op jit(solution)/shard_map/ppermute | solution.py:322
  17.7 14.7 %collective-permute-start.3 = (f32[400,128]{1,0:T(8,128)S(1)}, f32[400,128]{1,0:T(8,128)S(1)}, u32[]{:S(2)}, u32[]{:S(2)}) collective-permute-start(f32[400,128]{1,0:T(8,128)S(1)} %pad_maximum_fusion.1), channel_id=1, source_target_pairs={{0,12},{1,13},{2,14},{3,15},{4,8},{5,9},{6,10},{7,11},{8,4},{9,5},... | collective-permute-start | bytes 614408 | tf_op jit(solution)/shard_map/ppermute | solution.py:322
  32.5 3.3 %collective-permute-start.4 = (f32[1600,128]{1,0:T(8,128)S(1)}, f32[1600,128]{1,0:T(8,128)}, u32[]{:S(2)}, u32[]{:S(2)}) collective-permute-start(f32[1600,128]{1,0:T(8,128)S(1)} %constant_dynamic-update-slice_fusion.even_ref), channel_id=1, source_target_pairs={{0,1},{1,0},{2,3},{3,2},{4,5},{5,4},{6,7},{7,6},{8,9},{9,8},{10,11... | collective-permute-start | bytes 2457608 | tf_op jit(solution)/shard_map/ppermute | solution.py:325
  32.5 3.2 %copy-start.3 = (f32[5,64,512]{2,1,0:T(8,128)S(1)}, f32[5,64,512]{2,1,0:T(8,128)}, u32[]{:S(2)}) copy-start(f32[5,64,512]{2,1,0:T(8,128)} %q_ref.1) | copy-start | bytes 1966084
  35.7 1.1 %copy-start.1 = (f32[5,64,512]{2,1,0:T(8,128)S(1)}, f32[5,64,512]{2,1,0:T(8,128)}, u32[]{:S(2)}) copy-start(f32[5,64,512]{2,1,0:T(8,128)} %u_ref.1) | copy-start | bytes 1966084
  35.7 1.1 %copy-start.5 = (f32[64,512]{1,0:T(8,128)S(1)}, f32[64,512]{1,0:T(8,128)}, u32[]{:S(2)}) copy-start(f32[64,512]{1,0:T(8,128)} %v_ref.1) | copy-start | bytes 393220

commit v2 on v1

--- a/solution.py
+++ b/solution.py
@@ -75,9 +75,55 @@
     return up + jnp.where(row == SUB - 1, ghost, down)
 
 
+def fetch(pairs, sems):
+    copies = [pltpu.make_async_copy(src, dst, sems.at[n]) for n, (src, dst) in enumerate(pairs)]
+    for copy in copies:
+        copy.start()
+
+    def wait():
+        for copy in copies:
+            copy.wait()
+
+    return wait
+
+
+def edge_pairs(sz, state, source, viscosity, u_ref, q_ref, v_ref):
+    pairs = []
+    for n, first in enumerate((0, sz.rows - SUB)):
+        here = pl.ds(first, SUB)
+        pairs.append((state.at[:, here, :], u_ref.at[n]))
+        pairs.append((source.at[:, here, :], q_ref.at[n]))
+        pairs.append((viscosity.at[here, :], v_ref.at[n]))
+    return pairs
+
+
 def prepare_kernel(
-    sz, adv_ref, coup_ref, phase_ref, low_u, high_u, low_q, high_q, low_v, high_v, owner_ref, offset_ref, weight_ref, out_ref
+    sz,
+    adv_hbm,
+    coup_hbm,
+    phase_ref,
+    state_hbm,
+    source_hbm,
+    visc_hbm,
+    owner_hbm,
+    offset_hbm,
+    weight_hbm,
+    out_ref,
+    adv_ref,
+    coup_ref,
+    u_both,
+    q_both,
+    v_both,
+    owner_ref,
+    offset_ref,
+    weight_ref,
+    sems,
 ):
+    pairs = edge_pairs(sz, state_hbm, source_hbm, visc_hbm, u_both, q_both, v_both)
+    pairs += [(adv_hbm, adv_ref), (coup_hbm, coup_ref)]
+    pairs += [(owner_hbm, owner_ref), (offset_hbm, offset_ref), (weight_hbm, weight_ref)]
+    fetch(pairs, sems)()
+    (low_u, high_u), (low_q, high_q), (low_v, high_v) = [(r.at[0], r.at[1]) for r in (u_both, q_both, v_both)]
     own, speed = matrix_of(sz, adv_ref, coup_ref)
 
     def put(at, row):
@@ -139,13 +185,17 @@
     out_ref[sz.basis : sz.basis + 1, :] = jnp.where(used, basis, 0.0)
 
 
-def interior_kernel(sz, adv_ref, coup_ref, u_ref, q_ref, v_ref, out_ref, work):
+def interior_kernel(
+    sz, adv_hbm, coup_hbm, state_hbm, source_hbm, visc_hbm, out_hbm, adv_ref, coup_ref, u_ref, q_ref, v_ref, work, sems
+):
+    pairs = [(adv_hbm, adv_ref), (coup_hbm, coup_ref), (state_hbm, u_ref), (source_hbm, q_ref), (visc_hbm, v_ref)]
+    fetch(pairs, sems)()
     own, speed = matrix_of(sz, adv_ref, coup_ref)
     tiles = sz.rows // SUB
     row = lax.broadcasted_iota(jnp.int32, (SUB, sz.width), 0)
     for k in range(ITERS):
         src = u_ref if k == 0 else work.at[(k - 1) % 2]
-        dst = out_ref if k == ITERS - 1 else work.at[k % 2]
+        dst = work.at[k % 2]
         for t in range(tiles):
             here = slice(t * SUB, (t + 1) * SUB)
             u = [src[c, here, :] for c in range(sz.fields)]
@@ -159,22 +209,30 @@
             new = advance(sz, own, speed, u, PSEUDO * v_ref[here, :], column, lambda c: PSEUDO * q_ref[c, here, :])
             for c in range(sz.fields):
                 dst[c, here, :] = new[c]
+    fetch([(work.at[(ITERS - 1) % 2], out_hbm)], sems)()
 
 
 def couple_kernel(
     sz,
+    me_ref,
+    adv_hbm,
+    coup_hbm,
+    state_hbm,
+    source_hbm,
+    visc_hbm,
+    even_hbm,
+    odd_hbm,
+    inside_hbm,
+    out_hbm,
     adv_ref,
     coup_ref,
-    me_ref,
+    u_both,
+    q_both,
+    v_both,
     even_ref,
     odd_ref,
-    low_u,
-    high_u,
-    low_q,
-    high_q,
-    low_v,
-    high_v,
-    out_ref,
+    edge_ref,
+    sems,
     slot_offset,
     slot_weight,
     slot_value,
@@ -183,6 +241,12 @@
     lower_ref,
     bottom_ref,
 ):
+    pairs = [(even_hbm, even_ref), (odd_hbm, odd_ref), (adv_hbm, adv_ref), (coup_hbm, coup_ref)]
+    pairs += edge_pairs(sz, state_hbm, source_hbm, visc_hbm, u_both, q_both, v_both)
+    ends = [pl.ds(0, SUB), pl.ds(sz.rows - SUB, SUB)]
+    pairs += [(inside_hbm.at[:, here, :], edge_ref.at[n]) for n, here in enumerate(ends)]
+    fetch(pairs, sems)()
+    (low_u, high_u), (low_q, high_q), (low_v, high_v) = [(r.at[0], r.at[1]) for r in (u_both, q_both, v_both)]
     own, speed = matrix_of(sz, adv_ref, coup_ref)
     me = me_ref[0]
     packs, groups, fields = sz.packs, sz.groups, sz.fields
@@ -236,7 +300,7 @@
                 slot_value[o, c] = weight * pair[0] + (1.0 - weight) * pair[1]
             return carry
 
-        lax.fori_loop(0, sz.blocks, first_stage, 0, unroll=2)
+        lax.fori_loop(0, sz.blocks, first_stage, 0, unroll=min(sz.blocks, 16))
         for b in tiles:
             for g in range(groups):
                 cells = slice(g * LANES, (g + 1) * LANES)
@@ -250,7 +314,7 @@
                     )
 
                 zero = jnp.zeros((SUB, LANES), jnp.float32)
-                found = lax.fori_loop(0, sz.blocks, second_stage, (zero,) * fields, unroll=4)
+                found = lax.fori_loop(0, sz.blocks, second_stage, (zero,) * fields, unroll=min(sz.blocks, 16))
                 for c in range(fields):
                     lower_ref[b, c, :, cells] = found[c]
 
@@ -308,22 +372,31 @@
             state[at_low] = advance(
                 sz, own, speed, u, viscs[at_low], lambda c: edge_column(u[c], ghost[c], at_low), lambda c: PSEUDO * q[c]
             )
+    row = lax.broadcasted_iota(jnp.int32, (SUB, sz.width), 0)
     for c in range(fields):
-        out_ref[0, c] = state[True][c]
-        out_ref[1, c] = state[False][c]
+        edge_ref[0, c] = jnp.where(row < SUB // 2, state[True][c], edge_ref[0, c])
+        edge_ref[1, c] = jnp.where(row >= SUB // 2, state[False][c], edge_ref[1, c])
+    fetch([(edge_ref.at[n], out_hbm.at[:, here, :]) for n, here in enumerate(ends)], sems)()
 
 
 def spread(table, blocks):
-    parts = [table]
-    bit = 2
+    def swap(piece, mask):
+        return lax.ppermute(piece, "blk", [(i, i ^ mask) for i in range(blocks)])
+
+    parts, bit = [table], 4
     while bit < blocks:
-        masks = [bit] if bit == 2 or 2 * bit >= blocks else [bit, 2 * bit, 3 * bit]
-        have = jnp.concatenate(parts, axis=0)
-        parts = [have] + [lax.ppermute(have, "blk", [(i, i ^ m) for i in range(blocks)]) for m in masks]
+        masks = [bit, 2 * bit, 3 * bit] if 2 * bit < blocks else [bit]
+        have = jnp.concatenate(parts, axis=0) if len(parts) > 1 else parts[0]
+        parts = [have] + [swap(have, mask) for mask in masks]
         bit = bit * (len(masks) + 1)
-    even = jnp.concatenate(parts, axis=0)
-    odd = lax.ppermute(even, "blk", [(i, i ^ 1) for i in range(blocks)])
-    return even, odd
+    twos = [swap(part, 2) for part in parts]
+
+    def single(pieces):
+        size = table.shape[0]
+        return [piece[n : n + size] for piece in pieces for n in range(0, piece.shape[0], size)]
+
+    even = jnp.concatenate([t for pair in zip(single(parts), single(twos)) for t in pair], axis=0)
+    return even, swap(even, 1)
 
 
 def per_device(
@@ -339,54 +412,74 @@
 ):
     blocks = lax.axis_size("blk")
     fields, rows, width = state_now.shape
+    arrays = (state_now, time_source, viscosity, advection, coupling)
+    arrays += tuple(a.reshape(1, width) for a in (owner_list, owner_offset, intersection_weight))
+    arrays = [pltpu.with_memory_space_constraint(a, pltpu.HBM) for a in arrays]
+    state_now, time_source, viscosity, advection, coupling, owner_list, owner_offset, weight = arrays
     sz = Sizes(fields, rows, width, blocks)
     me = lax.axis_index("blk").astype(jnp.int32).reshape(1)
     smem = pl.BlockSpec(memory_space=pltpu.SMEM)
     vmem = pl.BlockSpec(memory_space=pltpu.VMEM)
-    ends = [
-        pl.BlockSpec((fields, SUB, width), lambda i: (0, 0, 0)),
-        pl.BlockSpec((fields, SUB, width), lambda i: (0, rows // SUB - 1, 0)),
+    hbm = pl.BlockSpec(memory_space=pltpu.HBM)
+    scalars = [pltpu.SMEM((fields,), jnp.float32), pltpu.SMEM((fields, fields), jnp.float32)]
+    edges = [
+        pltpu.VMEM((2, fields, SUB, width), jnp.float32),
+        pltpu.VMEM((2, fields, SUB, width), jnp.float32),
+        pltpu.VMEM((2, SUB, width), jnp.float32),
     ]
-    visc_ends = [
-        pl.BlockSpec((SUB, width), lambda i: (0, 0)),
-        pl.BlockSpec((SUB, width), lambda i: (rows // SUB - 1, 0)),
-    ]
-    edges = [state_now, state_now, time_source, time_source, viscosity, viscosity]
-    line = pl.BlockSpec((1, width), lambda i: (0, 0))
+    half = blocks // 2 * sz.table
+    block = jax.ShapeDtypeStruct((fields, rows, width), jnp.float32)
     limit = pltpu.CompilerParams(vmem_limit_bytes=50 * 1024 * 1024)
     table = pl.pallas_call(
         functools.partial(prepare_kernel, sz),
-        grid=(1,),
         out_shape=jax.ShapeDtypeStruct((sz.table, LANES), jnp.float32),
-        in_specs=[smem, smem, smem] + ends + ends + visc_ends + [line] * 3,
-        out_specs=pl.BlockSpec((sz.table, LANES), lambda i: (0, 0)),
+        in_specs=[hbm, hbm, smem] + [hbm] * 6,
+        out_specs=vmem,
+        scratch_shapes=scalars
+        + edges
+        + [pltpu.VMEM((1, width), kind) for kind in (jnp.int32, jnp.int32, jnp.float32)]
+        + [pltpu.SemaphoreType.DMA((11,))],
         compiler_params=limit,
     )(
         advection,
         coupling,
         phase_index,
-        *edges,
-        owner_list.reshape(1, width),
-        owner_offset.reshape(1, width),
-        intersection_weight.reshape(1, width),
+        state_now,
+        time_source,
+        viscosity,
+        owner_list,
+        owner_offset,
+        weight,
     )
     even, odd = spread(table, blocks)
     inside = pl.pallas_call(
         functools.partial(interior_kernel, sz),
-        out_shape=jax.ShapeDtypeStruct((fields, rows, width), jnp.float32),
-        in_specs=[smem, smem, vmem, vmem, vmem],
-        out_specs=vmem,
-        scratch_shapes=[pltpu.VMEM((2, fields, rows, width), jnp.float32)],
+        out_shape=block,
+        in_specs=[hbm] * 5,
+        out_specs=hbm,
+        scratch_shapes=scalars
+        + [
+            pltpu.VMEM((fields, rows, width), jnp.float32),
+            pltpu.VMEM((fields, rows, width), jnp.float32),
+            pltpu.VMEM((rows, width), jnp.float32),
+            pltpu.VMEM((2, fields, rows, width), jnp.float32),
+            pltpu.SemaphoreType.DMA((5,)),
+        ],
         compiler_params=limit,
     )(advection, coupling, state_now, time_source, viscosity)
-    whole = pl.BlockSpec((blocks // 2 * sz.table, LANES), lambda i: (0, 0))
-    strips = pl.pallas_call(
+    return pl.pallas_call(
         functools.partial(couple_kernel, sz),
-        grid=(1,),
-        out_shape=jax.ShapeDtypeStruct((2, fields, SUB, width), jnp.float32),
-        in_specs=[smem, smem, smem, whole, whole] + ends + ends + visc_ends,
-        out_specs=pl.BlockSpec((2, fields, SUB, width), lambda i: (0, 0, 0, 0)),
-        scratch_shapes=[
+        out_shape=block,
+        in_specs=[smem] + [hbm] * 8,
+        out_specs=hbm,
+        input_output_aliases={8: 0},
+        scratch_shapes=scalars
+        + edges
+        + [
+            pltpu.VMEM((half, LANES), jnp.float32),
+            pltpu.VMEM((half, LANES), jnp.float32),
+            pltpu.VMEM((2, fields, SUB, width), jnp.float32),
+            pltpu.SemaphoreType.DMA((12,)),
             pltpu.VMEM((blocks, SUB, LANES), jnp.int32),
             pltpu.VMEM((blocks, SUB, LANES), jnp.float32),
             pltpu.VMEM((blocks, fields, SUB, LANES), jnp.float32),
@@ -396,9 +489,7 @@
             pltpu.VMEM((fields, blocks, width), jnp.float32),
         ],
         compiler_params=limit,
-    )(advection, coupling, me, even, odd, *edges)
-    half = SUB // 2
-    return jnp.concatenate([strips[0, :, :half], inside[:, half : rows - half], strips[1, :, half:]], axis=1)
+    )(me, advection, coupling, state_now, time_source, viscosity, even, odd, inside)
 
 
 def solution(mesh):

time: 57.5 us -> 38.4 us (0.67)
  Pallas kernels: 23.6 us -> 16.5 us
  waiting for transfers between devices: 17.6 us -> 11.3 us
  local copies, waits for them, and re-layouts: 6.25 us -> 0.07 us
  starting transfers between devices: 7.63 us -> 9.52 us
  other arithmetic: 0.95 us -> 0 us
    pallas_call x3, Pallas kernels: 23.6 us -> 16.5 us  [the longest x1 10 us: per_device(): pl.pallas_call(functools.partial(couple_kernel, sz), out_shape=block, in_...]
    ppermute x5 -> x8, waiting for transfers between devices: 17.6 us -> 11.3 us  [swap(): return lax.ppermute(piece, 'blk', [(i, i ^ mask) for i in range(blocks)])]
    unnamed x26 -> x7, local copies, waits for them, and re-layouts: 6.15 us -> 0.06 us
    ppermute x5 -> x8, starting transfers between devices: 7.63 us -> 9.52 us  [swap(): return lax.ppermute(piece, 'blk', [(i, i ^ mask) for i in range(blocks)])]
    concatenate x2 -> x0, other arithmetic: 0.95 us -> none  [the longest x1 0.93 us: per_device(): jnp.concatenate([strips[0, :, :half], inside[:, half:rows - half], strips...]
  transfers between devices with their start and end apart: 5 -> 8, of which waited for: 3 -> 4; matrix products, arithmetic and copies ran while one was open for 0% -> 0% of each run, Pallas kernels for 5% -> 12%
where the time goes in v2:
time: 38.4 us; the launch traced here: 38.1 us
  Pallas kernels  16.5 us (43%)
  waiting for transfers between devices  11.3 us (29%)
  starting transfers between devices  9.52 us (25%)
  between operations  0.75 us (2%)
    ppermute x8, waiting for transfers between devices, swap(): return lax.ppermute(piece, 'blk', [(i, i ^ mask) for i in range(blocks)])  11.3 us
    pallas_call x1, Pallas kernels, per_device(): pl.pallas_call(functools.partial(couple_kernel, sz), out_shape=block, in_...  10 us
    ppermute x8, starting transfers between devices, swap(): return lax.ppermute(piece, 'blk', [(i, i ^ mask) for i in range(blocks)])  9.52 us
    pallas_call x1, Pallas kernels, per_device(): pl.pallas_call(functools.partial(interior_kernel, sz), out_shape=block, i...  4.51 us
    pallas_call x1, Pallas kernels, per_device(): pl.pallas_call(functools.partial(prepare_kernel, sz), out_shape=jax.Shape...  1.97 us
  transfers between devices with their start and end apart: 8, of which 4 were waited for; matrix products, arithmetic and copies ran while one was open for 0% of the time, Pallas kernels for 12%

profile of v2, /device:TPU:0, one launch (start us, length us, event | category | flops | bytes accessed | tf_op | source)
XLA Modules:
  0.0 38.1 jit_solution(1734768788503849362)
XLA Ops:
  0.7 2.0 %shard_map.91 = f32[200,128]{1,0:T(8,128)S(1)} custom-call(f32[5]{0:T(128)} %adv_hbm.5, f32[5,5]{1,0:T(8,128)} %coup_hbm.5, s32[1]{0:T(128)S(6)} %copy.19.phase_ref, f32[5,64,512]{2,1,0:T(8,128)} %state_hbm.5, f32[5,64,512]{2,1,0:T(8,128)} %source_hbm.5, f32[64,512]{1,0:T(8,128)} %visc_hbm.5, s32[1,512]{1,0:T(1,128)} %bitcast.4, s32[1,512]{1,0:T(1,128)} %bitcast.5, ...), custom_call_target="tpu_custom_call" | custom-call | tf_op jit(solution)/shard_map/pallas_call | solution.py:433
  2.6 3.0 %collective-permute-start = (f32[200,128]{1,0:T(8,128)S(1)}, f32[200,128]{1,0:T(8,128)S(1)}, u32[]{:S(2)}, u32[]{:S(2)}) collective-permute-start(f32[200,128]{1,0:T(8,128)S(1)} %shard_map.91), channel_id=1, source_target_pairs={{0,2},{1,3},{2,0},{3,1},{4,6},{5,7},{6,4},{7,5},{8,10},{9,11},{10,... | collective-permute-start | bytes 307208 | tf_op jit(solution)/shard_map/ppermute | solution.py:384
  5.7 1.6 %collective-permute-start.1 = (f32[200,128]{1,0:T(8,128)S(1)}, f32[200,128]{1,0:T(8,128)S(1)}, u32[]{:S(2)}, u32[]{:S(2)}) collective-permute-start(f32[200,128]{1,0:T(8,128)S(1)} %shard_map.91), channel_id=1, source_target_pairs={{0,4},{1,5},{2,6},{3,7},{4,0},{5,1},{6,2},{7,3},{8,12},{9,13},{10,... | collective-permute-start | bytes 307208 | tf_op jit(solution)/shard_map/ppermute | solution.py:384
  7.2 2.6 %collective-permute-start.3 = (f32[200,128]{1,0:T(8,128)S(1)}, f32[200,128]{1,0:T(8,128)S(1)}, u32[]{:S(2)}, u32[]{:S(2)}) collective-permute-start(f32[200,128]{1,0:T(8,128)S(1)} %shard_map.91), channel_id=1, source_target_pairs={{0,8},{1,9},{2,10},{3,11},{4,12},{5,13},{6,14},{7,15},{8,0},{9,1},... | collective-permute-start | bytes 307208 | tf_op jit(solution)/shard_map/ppermute | solution.py:384
  9.8 0.2 collective-permute-start.5
  10.1 1.3 %collective-permute-done.1 = f32[200,128]{1,0:T(8,128)S(1)} collective-permute-done((f32[200,128]{1,0:T(8,128)S(1)}, f32[200,128]{1,0:T(8,128)S(1)}, u32[]{:S(2)}, u32[]{:S(2)}) %collective-permute-start.1) | collective-permute-done | bytes 102432 | tf_op jit(solution)/shard_map/ppermute | solution.py:384
  11.3 0.0 collective-permute-start.2
  11.3 6.3 %collective-permute-done.3 = f32[200,128]{1,0:T(8,128)S(1)} collective-permute-done((f32[200,128]{1,0:T(8,128)S(1)}, f32[200,128]{1,0:T(8,128)S(1)}, u32[]{:S(2)}, u32[]{:S(2)}) %collective-permute-start.3) | collective-permute-done | bytes 102432 | tf_op jit(solution)/shard_map/ppermute | solution.py:384
  17.7 0.5 %collective-permute-start.4 = (f32[200,128]{1,0:T(8,128)S(1)}, f32[200,128]{1,0:T(8,128)S(1)}, u32[]{:S(2)}, u32[]{:S(2)}) collective-permute-start(f32[200,128]{1,0:T(8,128)S(1)} %collective-permute-done.3), channel_id=1, source_target_pairs={{0,2},{1,3},{2,0},{3,1},{4,6},{5,7},{6,4},{7,5},{8,10},{9,11},{10,... | collective-permute-start | bytes 307208 | tf_op jit(solution)/shard_map/ppermute | solution.py:384
  18.2 0.0 collective-permute-done.5
  18.2 1.5 %collective-permute-start.6 = (f32[200,128]{1,0:T(8,128)S(1)}, f32[200,128]{1,0:T(8,128)S(1)}, u32[]{:S(2)}, u32[]{:S(2)}) collective-permute-start(f32[200,128]{1,0:T(8,128)S(1)} %collective-permute-done.5), channel_id=1, source_target_pairs={{0,2},{1,3},{2,0},{3,1},{4,6},{5,7},{6,4},{7,5},{8,10},{9,11},{10,... | collective-permute-start | bytes 307208 | tf_op jit(solution)/shard_map/ppermute | solution.py:384
  19.7 0.0 collective-permute-done
  19.7 0.0 collective-permute-done.2
  19.8 2.6 %collective-permute-done.4 = f32[200,128]{1,0:T(8,128)S(1)} collective-permute-done((f32[200,128]{1,0:T(8,128)S(1)}, f32[200,128]{1,0:T(8,128)S(1)}, u32[]{:S(2)}, u32[]{:S(2)}) %collective-permute-start.4) | collective-permute-done | bytes 102432 | tf_op jit(solution)/shard_map/ppermute | solution.py:384
  22.4 1.1 %collective-permute-done.6 = f32[200,128]{1,0:T(8,128)S(1)} collective-permute-done((f32[200,128]{1,0:T(8,128)S(1)}, f32[200,128]{1,0:T(8,128)S(1)}, u32[]{:S(2)}, u32[]{:S(2)}) %collective-permute-start.6) | collective-permute-done | bytes 102432 | tf_op jit(solution)/shard_map/ppermute | solution.py:384
  23.5 0.1 collective-permute-start.7
  23.5 4.5 %shard_map.92.inside_hbm = f32[5,64,512]{2,1,0:T(8,128)} custom-call(f32[5]{0:T(128)} %adv_hbm.5, f32[5,5]{1,0:T(8,128)} %coup_hbm.5, f32[5,64,512]{2,1,0:T(8,128)} %state_hbm.5, f32[5,64,512]{2,1,0:T(8,128)} %source_hbm.5, f32[64,512]{1,0:T(8,128)} %visc_hbm.5), custom_call_target="tpu_custom_call" | custom-call | tf_op jit(solution)/shard_map/pallas_call | solution.py:455
  28.1 0.0 collective-permute-done.7.odd_hbm
  28.1 10.0 %shard_map.93 = f32[5,64,512]{2,1,0:T(8,128)} custom-call(s32[1]{0:T(128)} %bitcast.me_ref, f32[5]{0:T(128)} %adv_hbm.5, f32[5,5]{1,0:T(8,128)} %coup_hbm.5, f32[5,64,512]{2,1,0:T(8,128)} %state_hbm.5, f32[5,64,512]{2,1,0:T(8,128)} %source_hbm.5, f32[64,512]{1,0:T(8,128)} %visc_hbm.5, ...), custom_call_target="tpu_custom_call", output_to_operand_aliasing={{}: (8, {})} | custom-call | tf_op jit(solution)/shard_map/pallas_call | solution.py:470
  (8 shorter events, 0.1 us)
Async XLA Ops:
  2.6 17.1 %collective-permute-start = (f32[200,128]{1,0:T(8,128)S(1)}, f32[200,128]{1,0:T(8,128)S(1)}, u32[]{:S(2)}, u32[]{:S(2)}) collective-permute-start(f32[200,128]{1,0:T(8,128)S(1)} %shard_map.91), channel_id=1, source_target_pairs={{0,2},{1,3},{2,0},{3,1},{4,6},{5,7},{6,4},{7,5},{8,10},{9,11},{10,... | collective-permute-start | bytes 307208 | tf_op jit(solution)/shard_map/ppermute | solution.py:384
  5.7 5.7 %collective-permute-start.1 = (f32[200,128]{1,0:T(8,128)S(1)}, f32[200,128]{1,0:T(8,128)S(1)}, u32[]{:S(2)}, u32[]{:S(2)}) collective-permute-start(f32[200,128]{1,0:T(8,128)S(1)} %shard_map.91), channel_id=1, source_target_pairs={{0,4},{1,5},{2,6},{3,7},{4,0},{5,1},{6,2},{7,3},{8,12},{9,13},{10,... | collective-permute-start | bytes 307208 | tf_op jit(solution)/shard_map/ppermute | solution.py:384
  7.2 10.4 %collective-permute-start.3 = (f32[200,128]{1,0:T(8,128)S(1)}, f32[200,128]{1,0:T(8,128)S(1)}, u32[]{:S(2)}, u32[]{:S(2)}) collective-permute-start(f32[200,128]{1,0:T(8,128)S(1)} %shard_map.91), channel_id=1, source_target_pairs={{0,8},{1,9},{2,10},{3,11},{4,12},{5,13},{6,14},{7,15},{8,0},{9,1},... | collective-permute-start | bytes 307208 | tf_op jit(solution)/shard_map/ppermute | solution.py:384
  9.8 8.4 %collective-permute-start.5 = (f32[200,128]{1,0:T(8,128)S(1)}, f32[200,128]{1,0:T(8,128)S(1)}, u32[]{:S(2)}, u32[]{:S(2)}) collective-permute-start(f32[200,128]{1,0:T(8,128)S(1)} %shard_map.91), channel_id=1, source_target_pairs={{0,12},{1,13},{2,14},{3,15},{4,8},{5,9},{6,10},{7,11},{8,4},{9,5},... | collective-permute-start | bytes 307208 | tf_op jit(solution)/shard_map/ppermute | solution.py:384
  11.3 8.4 %collective-permute-start.2 = (f32[200,128]{1,0:T(8,128)S(1)}, f32[200,128]{1,0:T(8,128)S(1)}, u32[]{:S(2)}, u32[]{:S(2)}) collective-permute-start(f32[200,128]{1,0:T(8,128)S(1)} %collective-permute-done.1), channel_id=1, source_target_pairs={{0,2},{1,3},{2,0},{3,1},{4,6},{5,7},{6,4},{7,5},{8,10},{9,11},{10,... | collective-permute-start | bytes 307208 | tf_op jit(solution)/shard_map/ppermute | solution.py:384
  17.7 4.7 %collective-permute-start.4 = (f32[200,128]{1,0:T(8,128)S(1)}, f32[200,128]{1,0:T(8,128)S(1)}, u32[]{:S(2)}, u32[]{:S(2)}) collective-permute-start(f32[200,128]{1,0:T(8,128)S(1)} %collective-permute-done.3), channel_id=1, source_target_pairs={{0,2},{1,3},{2,0},{3,1},{4,6},{5,7},{6,4},{7,5},{8,10},{9,11},{10,... | collective-permute-start | bytes 307208 | tf_op jit(solution)/shard_map/ppermute | solution.py:384
  18.2 5.2 %collective-permute-start.6 = (f32[200,128]{1,0:T(8,128)S(1)}, f32[200,128]{1,0:T(8,128)S(1)}, u32[]{:S(2)}, u32[]{:S(2)}) collective-permute-start(f32[200,128]{1,0:T(8,128)S(1)} %collective-permute-done.5), channel_id=1, source_target_pairs={{0,2},{1,3},{2,0},{3,1},{4,6},{5,7},{6,4},{7,5},{8,10},{9,11},{10,... | collective-permute-start | bytes 307208 | tf_op jit(solution)/shard_map/ppermute | solution.py:384
  23.5 4.6 %collective-permute-start.7 = (f32[1600,128]{1,0:T(8,128)S(1)}, f32[1600,128]{1,0:T(8,128)S(1)}, u32[]{:S(2)}, u32[]{:S(2)}) collective-permute-start(f32[1600,128]{1,0:T(8,128)S(1)} %constant_dynamic-update-slice_fusion.even_hbm), channel_id=1, source_target_pairs={{0,1},{1,0},{2,3},{3,2},{4,5},{5,4},{6,7},{7,6},{8,9},{9,8},{10,11... | collective-permute-start | bytes 2457608 | tf_op jit(solution)/shard_map/ppermute | solution.py:384

commit v3 on v2

v3 whole, which is shorter than its diff:
```python
import functools
import math

import jax
import jax.numpy as jnp
from jax import lax
from jax.experimental import pallas as pl
from jax.experimental.pallas import tpu as pltpu
from jax.sharding import PartitionSpec as P

HARM = 8
PHASES = 512
LAG = 37
ITERS = 4
PSEUDO = 0.2
LANES = 128
SUB = 8
EXACT = lax.Precision.HIGHEST


class Sizes:
    def __init__(self, fields, rows, width, blocks):
        self.fields, self.rows, self.width, self.blocks = fields, rows, width, blocks
        self.groups = width // LANES
        self.cap = 2 * width // blocks
        self.packs = LANES // self.cap
        faces = fields * self.groups
        self.visc = 2 * faces
        self.slot = self.visc + 4 * self.groups
        self.offsets = self.slot + self.groups
        self.weights = self.offsets + SUB
        self.terms = self.weights + SUB
        self.basis = self.terms + 1
        self.first = -(-(self.basis + 1) // SUB) * SUB
        self.rest = -(-2 * (ITERS - 1) * faces // SUB) * SUB

        self.table = self.first + self.rest

    def top(self, k, c):
        return (2 * max(k - 1, 0) * self.fields + c) * self.groups

    def bottom(self, k, c):
        return self.top(k, c) + self.fields * self.groups


def matrix_of(sz, advection, coupling):
    own = [[-PSEUDO * coupling[c, d] for d in range(sz.fields)] for c in range(sz.fields)]
    speed = [PSEUDO * advection[c] for c in range(sz.fields)]
    for c in range(sz.fields):
        own[c][c] = own[c][c] + ((1.0 - 1.5 * PSEUDO) - speed[c])
    return own, speed


def shifted_west(u):
    lane = lax.broadcasted_iota(jnp.int32, u.shape, 1)
    return jnp.where(lane == 0, 0.0, pltpu.roll(u, 1, axis=1))


def shifted_east(u):
    width = u.shape[1]
    lane = lax.broadcasted_iota(jnp.int32, u.shape, 1)
    return jnp.where(lane == width - 1, 0.0, pltpu.roll(u, width - 1, axis=1))


def advance(sz, own, speed, u, visc, column, source):
    out = []
    for c in range(sz.fields):
        west, east = shifted_west(u[c]), shifted_east(u[c])
        new = speed[c] * west + visc * (west + east + column(c) - 4.0 * u[c])
        for d in range(sz.fields):
            new = new + own[c][d] * u[d]
        if source is not None:
            new = new - source(c)
        out.append(new)
    return out


def edge_column(u, ghost, at_low):
    row = lax.broadcasted_iota(jnp.int32, u.shape, 0)
    up, down = pltpu.roll(u, 1, axis=0), pltpu.roll(u, SUB - 1, axis=0)
    if at_low:
        return jnp.where(row == 0, ghost, up) + down
    return up + jnp.where(row == SUB - 1, ghost, down)


def fetch(pairs, sems):
    copies = [pltpu.make_async_copy(src, dst, sems.at[n]) for n, (src, dst) in enumerate(pairs)]
    for copy in copies:
        copy.start()

    def wait():
        for copy in copies:
            copy.wait()

    return wait


def edge_pairs(sz, state, source, viscosity, u_ref, q_ref, v_ref):
    pairs = []
    for n, first in enumerate((0, sz.rows - SUB)):
        here = pl.ds(first, SUB)
        pairs.append((state.at[:, here, :], u_ref.at[n]))
        pairs.append((source.at[:, here, :], q_ref.at[n]))
        pairs.append((viscosity.at[here, :], v_ref.at[n]))
    return pairs


def put(out_ref, at, row):
    for g in range(row.shape[1] // LANES):
        out_ref[at + g : at + g + 1, :] = row[:, g * LANES : (g + 1) * LANES]


def table_kernel(
    sz,
    phase_ref,
    adv_hbm,
    coup_hbm,
    state_hbm,
    source_hbm,
    visc_hbm,
    owner_hbm,
    offset_hbm,
    weight_hbm,
    out_ref,
    adv_ref,
    coup_ref,
    u_both,
    q_both,
    v_both,
    owner_ref,
    offset_ref,
    weight_ref,
    sems,
):
    pairs = [(owner_hbm, owner_ref), (offset_hbm, offset_ref), (weight_hbm, weight_ref)]
    pairs += edge_pairs(sz, state_hbm, source_hbm, visc_hbm, u_both, q_both, v_both)
    pairs += [(adv_hbm, adv_ref), (coup_hbm, coup_ref)]
    arrived = fetch(pairs, sems)
    out_ref[sz.terms : sz.first, :] = jnp.zeros((sz.first - sz.terms, LANES), jnp.float32)
    order = lax.broadcasted_iota(jnp.int32, (1, LANES), 1)
    harmonic = jnp.where(order > HARM, order - HARM, order).astype(jnp.float32)
    used = order <= 2 * HARM

    def waves(angle):
        product = angle * harmonic
        return jnp.where(order <= HARM, jnp.cos(product), jnp.sin(product))

    phase = phase_ref[0].astype(jnp.float32)
    scale = jnp.where(order == 0, 1.0, 2.0) / sz.blocks
    terms = waves(phase * (2.0 * math.pi / PHASES)) * scale
    basis = waves((phase + LAG) * (2.0 * math.pi / PHASES))
    out_ref[sz.terms : sz.terms + 1, :] = jnp.where(used, terms, 0.0)
    out_ref[sz.basis : sz.basis + 1, :] = jnp.where(used, basis, 0.0)
    before = lax.broadcasted_iota(jnp.int32, (sz.width, sz.width), 0) <= lax.broadcasted_iota(
        jnp.int32, (sz.width, sz.width), 1
    )
    before = before.astype(jnp.bfloat16)
    arrived()
    for c in range(sz.fields):
        put(out_ref, sz.top(0, c), u_both[1, c, SUB - 1 : SUB, :])
        put(out_ref, sz.bottom(0, c), u_both[0, c, 0:1, :])
    for n, (end, at) in enumerate(((1, SUB - 1), (1, SUB - 2), (0, 0), (0, 1))):
        put(out_ref, sz.visc + n * sz.groups, PSEUDO * v_both[end, at : at + 1, :])

    owner, offset, weight = owner_ref[...], offset_ref[...], weight_ref[...]
    member = lax.broadcasted_iota(jnp.int32, (sz.blocks, sz.width), 0) == owner
    member = member.astype(jnp.bfloat16)
    count = jnp.dot(member, before, preferred_element_type=jnp.float32)
    rank = jnp.sum(count * member.astype(jnp.float32), axis=0, keepdims=True) - 1.0
    rank = rank.astype(jnp.int32)
    slot = owner * sz.cap + rank
    put(out_ref, sz.slot, slot.astype(jnp.float32))
    place = (lax.broadcasted_iota(jnp.int32, (LANES, sz.width), 0) == slot % LANES).astype(jnp.float32)
    held = lax.broadcasted_iota(jnp.int32, (SUB, sz.width), 0) == slot // LANES
    values = jnp.concatenate(
        [jnp.where(held, offset.astype(jnp.float32), 0.0), jnp.where(held, weight, 0.0)], axis=0
    )
    out_ref[sz.offsets : sz.offsets + 2 * SUB, :] = lax.dot_general(
        values, place, (((1,), (1,)), ((), ())), precision=EXACT, preferred_element_type=jnp.float32
    )

    own, speed = matrix_of(sz, adv_ref, coup_ref)
    for end in range(2):
        at_low = end == 0
        face = 0 if at_low else SUB - 1
        visc = PSEUDO * v_both[end]
        u = [u_both[end, c] for c in range(sz.fields)]
        for k in range(1, ITERS):
            u = advance(
                sz, own, speed, u, visc, lambda c: edge_column(u[c], 0.0, at_low), lambda c: PSEUDO * q_both[end, c]
            )
            for c in range(sz.fields):
                put(out_ref, sz.first + (sz.bottom if at_low else sz.top)(k, c), u[c][face : face + 1])


def interior_kernel(
    sz,
    adv_hbm,
    coup_hbm,
    state_hbm,
    source_hbm,
    visc_hbm,
    after,
    out_hbm,
    passed,
    adv_ref,
    coup_ref,
    u_ref,
    q_ref,
    v_ref,
    work,
    sems,
):
    del after, passed
    pairs = [(adv_hbm, adv_ref), (coup_hbm, coup_ref), (state_hbm, u_ref), (source_hbm, q_ref), (visc_hbm, v_ref)]
    fetch(pairs, sems)()
    own, speed = matrix_of(sz, adv_ref, coup_ref)
    tiles = sz.rows // SUB
    row = lax.broadcasted_iota(jnp.int32, (SUB, sz.width), 0)
    for k in range(ITERS):
        src = u_ref if k == 0 else work.at[(k - 1) % 2]
        dst = work.at[k % 2]
        for t in range(tiles):
            here = slice(t * SUB, (t + 1) * SUB)
            u = [src[c, here, :] for c in range(sz.fields)]

            def column(c):
                up, down = pltpu.roll(u[c], 1, axis=0), pltpu.roll(u[c], SUB - 1, axis=0)
                above = src[c, t * SUB - 1 : t * SUB, :] if t > 0 else 0.0
                below = src[c, (t + 1) * SUB : (t + 1) * SUB + 1, :] if t < tiles - 1 else 0.0
                return jnp.where(row == 0, above, up) + jnp.where(row == SUB - 1, below, down)

            new = advance(sz, own, speed, u, PSEUDO * v_ref[here, :], column, lambda c: PSEUDO * q_ref[c, here, :])
            for c in range(sz.fields):
                dst[c, here, :] = new[c]
    fetch([(work.at[(ITERS - 1) % 2], out_hbm)], sems)()


def faces_of(sz, even_ref, odd_ref, base):
    def line(b, row):
        ref = (even_ref, odd_ref)[b % 2]
        return ref[pl.ds(b // 2 * sz.table + base + row, SUB, stride=sz.packs // 2 * sz.table), :]

    def wide(b, row):
        return jnp.concatenate([line(b, row + g) for g in range(sz.groups)], axis=1)

    return line, wide


def keep_faces(sz, b, c, top, bottom, top_ref, next_ref, bottom_ref):
    rows = pl.ds(b * SUB + c, SUB, stride=sz.packs * SUB)
    after = pltpu.roll(top, sz.width - 1, axis=1)
    for g in range(sz.groups):
        cells = slice(g * LANES, (g + 1) * LANES)
        top_ref.reshape(sz.groups, sz.blocks * SUB, LANES)[g, rows, :] = top[:, cells]
        next_ref.reshape(sz.groups, sz.blocks * SUB, LANES)[g, rows, :] = after[:, cells]
    bottom_ref[c, b * SUB : (b + 1) * SUB, :] = bottom


def gather(sz, slot_offset, slot_weight, slot_value, top_ref, next_ref, taker_ref, place_ref, lower_ref):
    fields, groups = sz.fields, sz.groups
    unroll = min(sz.blocks, 16)

    def first_stage(o, carry):
        offset, weight = slot_offset[o], slot_weight[o]
        at, part = offset % LANES, offset // LANES
        for c in range(fields):
            pair = []
            for ref in (top_ref, next_ref):
                value = None
                for g in range(groups):
                    source = jnp.broadcast_to(ref[g, o, c : c + 1, :], (SUB, LANES))
                    taken = jnp.take_along_axis(source, at, axis=1)
                    value = taken if value is None else jnp.where(part == g, taken, value)
                pair.append(value)
            slot_value[o, c] = weight * pair[0] + (1.0 - weight) * pair[1]
        return carry

    lax.fori_loop(0, sz.blocks, first_stage, 0, unroll=unroll)
    for b in range(sz.packs):
        for g in range(groups):
            cells = slice(g * LANES, (g + 1) * LANES)
            taker, place = taker_ref[b, :, cells], place_ref[b, :, cells]

            def second_stage(o, found):
                mine = taker == o
                return tuple(
                    jnp.where(mine, jnp.take_along_axis(slot_value[o, c], place, axis=1), found[c])
                    for c in range(fields)
                )

            zero = jnp.zeros((SUB, LANES), jnp.float32)
            found = lax.fori_loop(0, sz.blocks, second_stage, (zero,) * fields, unroll=unroll)
            for c in range(fields):
                lower_ref[b, c, :, cells] = found[c]


def gather_own(sz, own_offset, own_weight, top_ref, next_ref, taker, place):
    fields, groups, packs = sz.fields, sz.groups, sz.packs
    lane = lax.broadcasted_iota(jnp.int32, (SUB, LANES), 1)
    at, part = own_offset % LANES, own_offset // LANES

    def stacked(row):
        parts = [row[:, g * LANES : (g + 1) * LANES] for g in range(groups)]
        return jnp.concatenate(parts + [parts[0]] * (SUB - groups), axis=0)

    taker, place = stacked(taker), stacked(place)
    place = place + taker % packs * sz.cap
    ghost = []
    for c in range(fields):
        pair = []
        for ref in (top_ref, next_ref):
            value = jnp.zeros((SUB, LANES), jnp.float32)
            for b in range(packs):
                rows = pl.ds(b * SUB + c, SUB, stride=packs * SUB)
                for g in range(groups):
                    source = ref.reshape(groups, sz.blocks * SUB, LANES)[g, rows, :]
                    here = (part == g) & (lane // sz.cap == b)
                    value = jnp.where(here, jnp.take_along_axis(source, at, axis=1), value)
            pair.append(value)
        held = own_weight * pair[0] + (1.0 - own_weight) * pair[1]
        found = jnp.zeros((SUB, LANES), jnp.float32)
        for m in range(SUB):
            source = jnp.broadcast_to(held[m : m + 1], (SUB, LANES))
            found = jnp.where(taker // packs == m, jnp.take_along_axis(source, place, axis=1), found)
        ghost.append(jnp.concatenate([found[g : g + 1] for g in range(groups)], axis=1))
    return ghost


def mixed(kernel, bottom_ref, fields):
    return [jnp.dot(kernel, bottom_ref[c], precision=EXACT, preferred_element_type=jnp.float32) for c in range(fields)]


def couple_first(
    sz,
    me,
    even_ref,
    odd_ref,
    slot_offset,
    slot_weight,
    own_offset,
    own_weight,
    taker_ref,
    place_ref,
    kernel_ref,
    visc_ref,
    outer_ref,
    ghost_ref,
    slot_value,
    top_ref,
    next_ref,
    lower_ref,
    bottom_ref,
):
    packs, groups, fields = sz.packs, sz.groups, sz.fields
    lane = lax.broadcasted_iota(jnp.int32, (SUB, LANES), 1)
    line, wide = faces_of(sz, even_ref, odd_ref, 0)
    for b in range(packs):
        for c in range(fields):
            top, bottom = wide(b, sz.top(0, c)), wide(b, sz.bottom(0, c))
            keep_faces(sz, b, c, top, bottom, top_ref, next_ref, bottom_ref)

    for m in range(SUB):
        offsets = [line(b, sz.offsets + m) for b in range(packs)]
        weights = [line(b, sz.weights + m) for b in range(packs)]
        for n in range(packs):
            tile_o, tile_w = offsets[n], weights[n]
            for b in range(packs):
                if b != n:
                    mine = lane // sz.cap == b
                    turn = (b - n) * sz.cap % LANES
                    tile_o = jnp.where(mine, pltpu.roll(offsets[b], turn, axis=1), tile_o)
                    tile_w = jnp.where(mine, pltpu.roll(weights[b], turn, axis=1), tile_w)
            o = jnp.bitwise_xor(m * packs + n, me)
            slot_offset[o] = tile_o.astype(jnp.int32)
            slot_weight[o] = tile_w
    for b in range(packs):
        slots = wide(b, sz.slot).astype(jnp.int32)
        taker_ref[b] = jnp.bitwise_xor(slots // sz.cap, me)
        place_ref[b] = slots % sz.cap + b * sz.cap
        for n in range(4):
            visc_ref[n, b] = wide(b, sz.visc + n * groups)
    basis = jnp.concatenate([line(b, sz.basis) for b in range(packs)], axis=0)
    terms = jnp.concatenate([line(b, sz.terms) for b in range(packs)], axis=0)
    kernel = lax.dot_general(
        basis, terms, (((1,), (1,)), ((), ())), precision=EXACT, preferred_element_type=jnp.float32
    )
    kernel_ref[...] = kernel

    sublane = lax.broadcasted_iota(jnp.int32, (SUB, LANES), 0)
    for ref, out in ((slot_offset, own_offset), (slot_weight, own_weight)):
        tile = jnp.zeros((SUB, LANES), out.dtype)
        for o in range(sz.blocks):
            here = (sublane == o // packs) & (lane // sz.cap == o % packs)
            turn = o % packs * sz.cap
            line_o = jnp.broadcast_to(ref[o, 0:1, :], (SUB, LANES))
            tile = jnp.where(here, pltpu.roll(line_o, turn, axis=1) if turn else line_o, tile)
        out[...] = tile

    upper = mixed(kernel, bottom_ref, fields)
    gather(sz, slot_offset, slot_weight, slot_value, top_ref, next_ref, taker_ref, place_ref, lower_ref)
    for c in range(fields):
        ghost_ref[0, c] = lower_ref[0, c]
        ghost_ref[1, c] = upper[c][0:SUB]
        for b in range(packs):
            outer_ref[0, b, c] = visc_ref[0, b] * upper[c][b * SUB : (b + 1) * SUB]
            outer_ref[1, b, c] = visc_ref[2, b] * lower_ref[b, c]


def couple_kernel(sz, me_ref, adv_hbm, coup_hbm, visc_hbm, even_ref, odd_ref, inside_hbm, out_hbm, *scratch):
    adv_ref, coup_ref, ends_ref, edge_ref, sems = scratch[:5]
    carried, work = scratch[5:-5], scratch[-5:]
    slot_offset, slot_weight, own_offset, own_weight, taker_ref, place_ref, kernel_ref, visc_ref, outer_ref, ghost_ref = carried
    slot_value, top_ref, next_ref, lower_ref, bottom_ref = work
    ends = [pl.ds(0, SUB), pl.ds(sz.rows - SUB, SUB)]
    pairs = [(adv_hbm, adv_ref), (coup_hbm, coup_ref)]
    pairs += [(visc_hbm.at[here, :], ends_ref.at[n]) for n, here in enumerate(ends)]
    pairs += [(inside_hbm.at[:, here, :], edge_ref.at[n]) for n, here in enumerate(ends)]
    arrived = fetch(pairs, sems)
    couple_first(sz, me_ref[0], even_ref, odd_ref, *carried, *work)
    packs, fields = sz.packs, sz.fields
    _, wide = faces_of(sz, even_ref, odd_ref, sz.first)
    kernel = kernel_ref[...]
    outer = {(n, b): [outer_ref[n, b, c] for c in range(fields)] for n in range(2) for b in range(packs)}
    inner = {}

    half = SUB // 2
    row = lax.broadcasted_iota(jnp.int32, (SUB, sz.width), 0)

    def ghosts_only(lower, upper):
        return [jnp.where(row == 0, lower[c], jnp.where(row == SUB - 1, upper[c], 0.0)) for c in range(fields)]

    for k in range(1, ITERS):
        for b in range(packs):
            for c in range(fields):
                top = wide(b, sz.top(k, c)) + outer[0, b][c]
                bottom = wide(b, sz.bottom(k, c)) + outer[1, b][c]
                keep_faces(sz, b, c, top, bottom, top_ref, next_ref, bottom_ref)
        if k == ITERS - 1:
            upper = mixed(kernel[:SUB], bottom_ref, fields)
            taker, place = taker_ref[0, 0:1, :], place_ref[0, 0:1, :]
            lower = gather_own(sz, own_offset[...], own_weight[...], top_ref, next_ref, taker, place)
        else:
            upper = mixed(kernel, bottom_ref, fields)
            gather(sz, slot_offset, slot_weight, slot_value, top_ref, next_ref, taker_ref, place_ref, lower_ref)
            lower = [lower_ref[0, c, 0:1, :] for c in range(fields)]
            if k == 1:
                arrived()
                own, speed = matrix_of(sz, adv_ref, coup_ref)
            for n in range(2):
                for b in range(packs):
                    e, e_in = outer[n, b], inner.get((n, b))
                    inner[n, b] = [visc_ref[2 * n + 1, b] * e[c] for c in range(fields)]

                    def column(c):
                        next_to = upper[c][b * SUB : (b + 1) * SUB] if n == 0 else lower_ref[b, c]
                        return next_to if e_in is None else next_to + e_in[c]

                    outer[n, b] = advance(sz, own, speed, e, visc_ref[2 * n, b], column, None)
        if k == 1:
            visc = PSEUDO * jnp.where(row < half, ends_ref[0], ends_ref[1])
            firsts = [[ghost_ref[n, c, 0:1, :] for c in range(fields)] for n in range(2)]
            forced = [visc * g for g in ghosts_only(*firsts)]
        ghost = ghosts_only(lower, [upper[c][0:1] for c in range(fields)])

        def around(c):
            up = jnp.where((row == 0) | (row == half), 0.0, pltpu.roll(forced[c], 1, axis=0))
            down = jnp.where((row == SUB - 1) | (row == half - 1), 0.0, pltpu.roll(forced[c], SUB - 1, axis=0))
            return up + down + ghost[c]

        forced = advance(sz, own, speed, forced, visc, around, None)
    for c in range(fields):
        edge_ref[0, c] = edge_ref[0, c] + jnp.where(row < half, forced[c], 0.0)
        edge_ref[1, c] = edge_ref[1, c] + jnp.where(row >= half, forced[c], 0.0)
    fetch([(edge_ref.at[n], out_hbm.at[:, here, :]) for n, here in enumerate(ends)], sems)()


def spread(table, blocks, between):
    def swap(piece, mask):
        return lax.ppermute(piece, "blk", [(i, i ^ mask) for i in range(blocks)])

    parts, bit = [table], 4
    while bit < blocks:
        masks = [bit, 2 * bit, 3 * bit] if 2 * bit < blocks else [bit]
        have = jnp.concatenate(parts, axis=0) if len(parts) > 1 else parts[0]
        parts = [have] + [swap(have, mask) for mask in masks]
        bit = bit * (len(masks) + 1)
    parts[1] = between(parts[1])
    twos = [swap(part, 2) for part in parts]
    even = jnp.concatenate([t for pair in zip(parts, twos) for t in pair], axis=0)
    return even, swap(even, 1)


def per_device(
    state_now,
    time_source,
    viscosity,
    advection,
    coupling,
    owner_list,
    owner_offset,
    intersection_weight,
    phase_index,
):
    blocks = lax.axis_size("blk")
    fields, rows, width = state_now.shape
    arrays = (state_now, time_source, viscosity, advection, coupling)
    arrays += tuple(a.reshape(1, width) for a in (owner_list, owner_offset, intersection_weight))
    arrays = [pltpu.with_memory_space_constraint(a, pltpu.HBM) for a in arrays]
    state_now, time_source, viscosity, advection, coupling, owner_list, owner_offset, weight = arrays
    sz = Sizes(fields, rows, width, blocks)
    me = lax.axis_index("blk").astype(jnp.int32).reshape(1)
    smem = pl.BlockSpec(memory_space=pltpu.SMEM)
    vmem = pl.BlockSpec(memory_space=pltpu.VMEM)
    hbm = pl.BlockSpec(memory_space=pltpu.HBM)
    anywhere = pl.BlockSpec(memory_space=pl.ANY)
    f32, i32 = jnp.float32, jnp.int32
    scalars = [pltpu.SMEM((fields,), f32), pltpu.SMEM((fields, fields), f32)]
    block = jax.ShapeDtypeStruct((fields, rows, width), f32)
    limit = pltpu.CompilerParams(vmem_limit_bytes=50 * 1024 * 1024)
    two_ends = pltpu.VMEM((2, fields, SUB, width), f32)
    visc_ends = pltpu.VMEM((2, SUB, width), f32)
    table = pl.pallas_call(
        functools.partial(table_kernel, sz),
        out_shape=jax.ShapeDtypeStruct((sz.table, LANES), f32),
        in_specs=[smem] + [hbm] * 8,
        out_specs=vmem,
        scratch_shapes=scalars
        + [two_ends, two_ends, visc_ends]
        + [pltpu.VMEM((1, width), kind) for kind in (i32, i32, f32)]
        + [pltpu.SemaphoreType.DMA((11,))],
        compiler_params=limit,
    )(phase_index, advection, coupling, state_now, time_source, viscosity, owner_list, owner_offset, weight)
    insides = []

    def interior(piece):
        inside, piece = pl.pallas_call(
            functools.partial(interior_kernel, sz),
            out_shape=[block, jax.ShapeDtypeStruct(piece.shape, piece.dtype)],
            in_specs=[hbm] * 5 + [anywhere],
            out_specs=[hbm, anywhere],
            input_output_aliases={5: 1},
            scratch_shapes=scalars
            + [
                pltpu.VMEM((fields, rows, width), f32),
                pltpu.VMEM((fields, rows, width), f32),
                pltpu.VMEM((rows, width), f32),
                pltpu.VMEM((2, fields, rows, width), f32),
                pltpu.SemaphoreType.DMA((5,)),
            ],
            compiler_params=limit,
        )(advection, coupling, state_now, time_source, viscosity, piece)
        insides.append(inside)
        return piece

    even, odd = spread(table, blocks, interior)
    work = [
        pltpu.VMEM((blocks, fields, SUB, LANES), f32),
        pltpu.VMEM((sz.groups, blocks, SUB, LANES), f32),
        pltpu.VMEM((sz.groups, blocks, SUB, LANES), f32),
        pltpu.VMEM((sz.packs, fields, SUB, width), f32),
        pltpu.VMEM((fields, blocks, width), f32),
    ]
    carried = [
        pltpu.VMEM((blocks, SUB, LANES), i32),
        pltpu.VMEM((blocks, SUB, LANES), f32),
        pltpu.VMEM((SUB, LANES), i32),
        pltpu.VMEM((SUB, LANES), f32),
        pltpu.VMEM((sz.packs, SUB, width), i32),
        pltpu.VMEM((sz.packs, SUB, width), i32),
        pltpu.VMEM((blocks, blocks), f32),
        pltpu.VMEM((4, sz.packs, SUB, width), f32),
        pltpu.VMEM((2, sz.packs, fields, SUB, width), f32),
        pltpu.VMEM((2, fields, SUB, width), f32),
    ]
    return pl.pallas_call(
        functools.partial(couple_kernel, sz),
        out_shape=block,
        in_specs=[smem] + [hbm] * 3 + [vmem] * 2 + [hbm],
        out_specs=hbm,
        input_output_aliases={6: 0},
        scratch_shapes=scalars + [visc_ends, two_ends, pltpu.SemaphoreType.DMA((6,))] + carried + work,
        compiler_params=limit,
    )(me, advection, coupling, viscosity, even, odd, insides[0])


def solution(mesh):
    return jax.shard_map(
        per_device,
        mesh=mesh,
        in_specs=(
            P(None, None, ("groups", "blk")),
            P(None, None, ("groups", "blk")),
            P(None, ("groups", "blk")),
            P(),
            P(),
            P(("groups", "blk"), None),
            P(("groups", "blk")),
            P(("groups", "blk")),
            P(("groups", "blk")),
        ),
        out_specs=P(None, None, ("groups", "blk")),
        check_vma=False,
    )
```

time: 38.4 us -> 33.6 us (0.88)
  Pallas kernels: 16.5 us -> 14 us
  waiting for transfers between devices: 11.3 us -> 8.99 us
    pallas_call x1, Pallas kernels: 10 us -> 7.52 us  [per_device(): pl.pallas_call(functools.partial(couple_kernel, sz), out_shape=block, in_...]
    ppermute x8, waiting for transfers between devices: 11.3 us -> 8.99 us  [swap(): return lax.ppermute(piece, 'blk', [(i, i ^ mask) for i in range(blocks)])]
  transfers between devices with their start and end apart: 8 -> 8, of which waited for: 4 -> 6; matrix products, arithmetic and copies ran while one was open for 0% -> 0% of each run, Pallas kernels for 12% -> 13%
where the time goes in v3:
time: 33.6 us; the launch traced here: 33.4 us
  Pallas kernels  14 us (42%)
  starting transfers between devices  9.59 us (29%)
  waiting for transfers between devices  8.99 us (27%)
  between operations  0.73 us (2%)
    ppermute x8, starting transfers between devices, swap(): return lax.ppermute(piece, 'blk', [(i, i ^ mask) for i in range(blocks)])  9.59 us
    ppermute x8, waiting for transfers between devices, swap(): return lax.ppermute(piece, 'blk', [(i, i ^ mask) for i in range(blocks)])  8.99 us
    pallas_call x1, Pallas kernels, per_device(): pl.pallas_call(functools.partial(couple_kernel, sz), out_shape=block, in_...  7.52 us
    pallas_call x1, Pallas kernels, interior(): pl.pallas_call(functools.partial(interior_kernel, sz), out_shape=[block,...  4.51 us
    pallas_call x1, Pallas kernels, per_device(): pl.pallas_call(functools.partial(table_kernel, sz), out_shape=jax.ShapeDt...  2 us
  transfers between devices with their start and end apart: 8, of which 6 were waited for; matrix products, arithmetic and copies ran while one was open for 0% of the time, Pallas kernels for 13%

profile of v3, /device:TPU:0, one launch (start us, length us, event | category | flops | bytes accessed | tf_op | source)
XLA Modules:
  0.0 33.4 jit_solution(10148418832109108715)
XLA Ops:
  0.7 2.0 %shard_map.91 = f32[200,128]{1,0:T(8,128)S(1)} custom-call(s32[1]{0:T(128)S(6)} %copy.21.phase_ref, f32[5]{0:T(128)} %adv_hbm.5, f32[5,5]{1,0:T(8,128)} %coup_hbm.5, f32[5,64,512]{2,1,0:T(8,128)} %state_hbm.3, f32[5,64,512]{2,1,0:T(8,128)} %source_hbm.3, f32[64,512]{1,0:T(8,128)} %visc_hbm.5, s32[1,512]{1,0:T(1,128)} %bitcast.4, s32[1,512]{1,0:T(1,128)} %bitcast.5, ...), custom_call_target="tpu_custom_call" | custom-call | tf_op jit(solution)/shard_map/pallas_call | solution.py:523
  2.7 3.0 %collective-permute-start = (f32[200,128]{1,0:T(8,128)S(1)}, f32[200,128]{1,0:T(8,128)S(1)}, u32[]{:S(2)}, u32[]{:S(2)}) collective-permute-start(f32[200,128]{1,0:T(8,128)S(1)} %shard_map.91), channel_id=1, source_target_pairs={{0,2},{1,3},{2,0},{3,1},{4,6},{5,7},{6,4},{7,5},{8,10},{9,11},{10,... | collective-permute-start | bytes 307208 | tf_op jit(solution)/shard_map/ppermute | solution.py:480
  5.7 1.6 %collective-permute-start.1 = (f32[200,128]{1,0:T(8,128)S(1)}, f32[200,128]{1,0:T(8,128)S(1)}, u32[]{:S(2)}, u32[]{:S(2)}) collective-permute-start(f32[200,128]{1,0:T(8,128)S(1)} %shard_map.91), channel_id=1, source_target_pairs={{0,4},{1,5},{2,6},{3,7},{4,0},{5,1},{6,2},{7,3},{8,12},{9,13},{10,... | collective-permute-start | bytes 307208 | tf_op jit(solution)/shard_map/ppermute | solution.py:480
  7.3 2.6 %collective-permute-start.3 = (f32[200,128]{1,0:T(8,128)S(1)}, f32[200,128]{1,0:T(8,128)S(1)}, u32[]{:S(2)}, u32[]{:S(2)}) collective-permute-start(f32[200,128]{1,0:T(8,128)S(1)} %shard_map.91), channel_id=1, source_target_pairs={{0,8},{1,9},{2,10},{3,11},{4,12},{5,13},{6,14},{7,15},{8,0},{9,1},... | collective-permute-start | bytes 307208 | tf_op jit(solution)/shard_map/ppermute | solution.py:480
  9.9 0.2 collective-permute-start.5
  10.1 1.3 %collective-permute-done.1.after = f32[200,128]{1,0:T(8,128)S(1)} collective-permute-done((f32[200,128]{1,0:T(8,128)S(1)}, f32[200,128]{1,0:T(8,128)S(1)}, u32[]{:S(2)}, u32[]{:S(2)}) %collective-permute-start.1) | collective-permute-done | bytes 102432 | tf_op jit(solution)/shard_map/ppermute | solution.py:480
  11.4 4.5 %shard_map.92 = (f32[5,64,512]{2,1,0:T(8,128)}, f32[200,128]{1,0:T(8,128)S(1)}) custom-call(f32[5]{0:T(128)} %adv_hbm.5, f32[5,5]{1,0:T(8,128)} %coup_hbm.5, f32[5,64,512]{2,1,0:T(8,128)} %state_hbm.3, f32[5,64,512]{2,1,0:T(8,128)} %source_hbm.3, f32[64,512]{1,0:T(8,128)} %visc_hbm.5, ...), custom_call_target="tpu_custom_call", output_to_operand_aliasing={{1}: (5, {})} | custom-call | tf_op jit(solution)/shard_map/pallas_call | solution.py:537
  15.9 0.1 collective-permute-start.2
  16.0 1.7 %collective-permute-done.3 = f32[200,128]{1,0:T(8,128)S(1)} collective-permute-done((f32[200,128]{1,0:T(8,128)S(1)}, f32[200,128]{1,0:T(8,128)S(1)}, u32[]{:S(2)}, u32[]{:S(2)}) %collective-permute-start.3) | collective-permute-done | bytes 102432 | tf_op jit(solution)/shard_map/ppermute | solution.py:480
  17.7 0.5 %collective-permute-start.4 = (f32[200,128]{1,0:T(8,128)S(1)}, f32[200,128]{1,0:T(8,128)S(1)}, u32[]{:S(2)}, u32[]{:S(2)}) collective-permute-start(f32[200,128]{1,0:T(8,128)S(1)} %collective-permute-done.3), channel_id=1, source_target_pairs={{0,2},{1,3},{2,0},{3,1},{4,6},{5,7},{6,4},{7,5},{8,10},{9,11},{10,... | collective-permute-start | bytes 307208 | tf_op jit(solution)/shard_map/ppermute | solution.py:480
  18.2 0.0 collective-permute-done.5
  18.2 1.5 %collective-permute-start.6 = (f32[200,128]{1,0:T(8,128)S(1)}, f32[200,128]{1,0:T(8,128)S(1)}, u32[]{:S(2)}, u32[]{:S(2)}) collective-permute-start(f32[200,128]{1,0:T(8,128)S(1)} %collective-permute-done.5), channel_id=1, source_target_pairs={{0,2},{1,3},{2,0},{3,1},{4,6},{5,7},{6,4},{7,5},{8,10},{9,11},{10,... | collective-permute-start | bytes 307208 | tf_op jit(solution)/shard_map/ppermute | solution.py:480
  19.8 0.0 collective-permute-done
  19.8 0.8 %collective-permute-done.2 = f32[200,128]{1,0:T(8,128)S(1)} collective-permute-done((f32[200,128]{1,0:T(8,128)S(1)}, f32[200,128]{1,0:T(8,128)S(1)}, u32[]{:S(2)}, u32[]{:S(2)}) %collective-permute-start.2) | collective-permute-done | bytes 102432 | tf_op jit(solution)/shard_map/ppermute | solution.py:480
  20.6 1.7 %collective-permute-done.4 = f32[200,128]{1,0:T(8,128)S(1)} collective-permute-done((f32[200,128]{1,0:T(8,128)S(1)}, f32[200,128]{1,0:T(8,128)S(1)}, u32[]{:S(2)}, u32[]{:S(2)}) %collective-permute-start.4) | collective-permute-done | bytes 102432 | tf_op jit(solution)/shard_map/ppermute | solution.py:480
  22.4 1.1 %collective-permute-done.6 = f32[200,128]{1,0:T(8,128)S(1)} collective-permute-done((f32[200,128]{1,0:T(8,128)S(1)}, f32[200,128]{1,0:T(8,128)S(1)}, u32[]{:S(2)}, u32[]{:S(2)}) %collective-permute-start.6) | collective-permute-done | bytes 102432 | tf_op jit(solution)/shard_map/ppermute | solution.py:480
  23.5 0.1 collective-permute-start.7
  23.6 2.3 %collective-permute-done.7.odd_ref = f32[1600,128]{1,0:T(8,128)S(1)} collective-permute-done((f32[1600,128]{1,0:T(8,128)S(1)}, f32[1600,128]{1,0:T(8,128)S(1)}, u32[]{:S(2)}, u32[]{:S(2)}) %collective-permute-start.7) | collective-permute-done | bytes 819232 | tf_op jit(solution)/shard_map/ppermute | solution.py:480
  25.9 7.5 %shard_map.93 = f32[5,64,512]{2,1,0:T(8,128)} custom-call(s32[1]{0:T(128)} %bitcast.me_ref, f32[5]{0:T(128)} %adv_hbm.5, f32[5,5]{1,0:T(8,128)} %coup_hbm.5, f32[64,512]{1,0:T(8,128)} %visc_hbm.5, f32[1600,128]{1,0:T(8,128)S(1)} %constant_dynamic-update-slice_fusion.even_ref, ...), custom_call_target="tpu_custom_call", output_to_operand_aliasing={{}: (6, {})} | custom-call | tf_op jit(solution)/shard_map/pallas_call | solution.py:576
  (8 shorter events, 0.1 us)
Async XLA Ops:
  2.7 17.1 %collective-permute-start = (f32[200,128]{1,0:T(8,128)S(1)}, f32[200,128]{1,0:T(8,128)S(1)}, u32[]{:S(2)}, u32[]{:S(2)}) collective-permute-start(f32[200,128]{1,0:T(8,128)S(1)} %shard_map.91), channel_id=1, source_target_pairs={{0,2},{1,3},{2,0},{3,1},{4,6},{5,7},{6,4},{7,5},{8,10},{9,11},{10,... | collective-permute-start | bytes 307208 | tf_op jit(solution)/shard_map/ppermute | solution.py:480
  5.7 5.7 %collective-permute-start.1 = (f32[200,128]{1,0:T(8,128)S(1)}, f32[200,128]{1,0:T(8,128)S(1)}, u32[]{:S(2)}, u32[]{:S(2)}) collective-permute-start(f32[200,128]{1,0:T(8,128)S(1)} %shard_map.91), channel_id=1, source_target_pairs={{0,4},{1,5},{2,6},{3,7},{4,0},{5,1},{6,2},{7,3},{8,12},{9,13},{10,... | collective-permute-start | bytes 307208 | tf_op jit(solution)/shard_map/ppermute | solution.py:480
  7.3 10.4 %collective-permute-start.3 = (f32[200,128]{1,0:T(8,128)S(1)}, f32[200,128]{1,0:T(8,128)S(1)}, u32[]{:S(2)}, u32[]{:S(2)}) collective-permute-start(f32[200,128]{1,0:T(8,128)S(1)} %shard_map.91), channel_id=1, source_target_pairs={{0,8},{1,9},{2,10},{3,11},{4,12},{5,13},{6,14},{7,15},{8,0},{9,1},... | collective-permute-start | bytes 307208 | tf_op jit(solution)/shard_map/ppermute | solution.py:480
  9.9 8.4 %collective-permute-start.5 = (f32[200,128]{1,0:T(8,128)S(1)}, f32[200,128]{1,0:T(8,128)S(1)}, u32[]{:S(2)}, u32[]{:S(2)}) collective-permute-start(f32[200,128]{1,0:T(8,128)S(1)} %shard_map.91), channel_id=1, source_target_pairs={{0,12},{1,13},{2,14},{3,15},{4,8},{5,9},{6,10},{7,11},{8,4},{9,5},... | collective-permute-start | bytes 307208 | tf_op jit(solution)/shard_map/ppermute | solution.py:480
  15.9 4.7 %collective-permute-start.2 = (f32[200,128]{1,0:T(8,128)S(1)}, f32[200,128]{1,0:T(8,128)S(1)}, u32[]{:S(2)}, u32[]{:S(2)}) collective-permute-start(f32[200,128]{1,0:T(8,128)S(1)} %get-tuple-element.7), channel_id=1, source_target_pairs={{0,2},{1,3},{2,0},{3,1},{4,6},{5,7},{6,4},{7,5},{8,10},{9,11},{10,... | collective-permute-start | bytes 307208 | tf_op jit(solution)/shard_map/ppermute | solution.py:480
  17.7 4.7 %collective-permute-start.4 = (f32[200,128]{1,0:T(8,128)S(1)}, f32[200,128]{1,0:T(8,128)S(1)}, u32[]{:S(2)}, u32[]{:S(2)}) collective-permute-start(f32[200,128]{1,0:T(8,128)S(1)} %collective-permute-done.3), channel_id=1, source_target_pairs={{0,2},{1,3},{2,0},{3,1},{4,6},{5,7},{6,4},{7,5},{8,10},{9,11},{10,... | collective-permute-start | bytes 307208 | tf_op jit(solution)/shard_map/ppermute | solution.py:480
  18.2 5.2 %collective-permute-start.6 = (f32[200,128]{1,0:T(8,128)S(1)}, f32[200,128]{1,0:T(8,128)S(1)}, u32[]{:S(2)}, u32[]{:S(2)}) collective-permute-start(f32[200,128]{1,0:T(8,128)S(1)} %collective-permute-done.5), channel_id=1, source_target_pairs={{0,2},{1,3},{2,0},{3,1},{4,6},{5,7},{6,4},{7,5},{8,10},{9,11},{10,... | collective-permute-start | bytes 307208 | tf_op jit(solution)/shard_map/ppermute | solution.py:480
  23.5 2.4 %collective-permute-start.7 = (f32[1600,128]{1,0:T(8,128)S(1)}, f32[1600,128]{1,0:T(8,128)S(1)}, u32[]{:S(2)}, u32[]{:S(2)}) collective-permute-start(f32[1600,128]{1,0:T(8,128)S(1)} %constant_dynamic-update-slice_fusion.even_ref), channel_id=1, source_target_pairs={{0,1},{1,0},{2,3},{3,2},{4,5},{5,4},{6,7},{7,6},{8,9},{9,8},{10,11... | collective-permute-start | bytes 2457608 | tf_op jit(solution)/shard_map/ppermute | solution.py:480

commit v4 on v3

--- a/solution.py
+++ b/solution.py
@@ -75,12 +75,20 @@
     return out
 
 
-def edge_column(u, ghost, at_low):
+def inside_column(u):
     row = lax.broadcasted_iota(jnp.int32, u.shape, 0)
-    up, down = pltpu.roll(u, 1, axis=0), pltpu.roll(u, SUB - 1, axis=0)
-    if at_low:
-        return jnp.where(row == 0, ghost, up) + down
-    return up + jnp.where(row == SUB - 1, ghost, down)
+    half = SUB // 2
+    up = jnp.where((row == 0) | (row == half), 0.0, pltpu.roll(u, 1, axis=0))
+    down = jnp.where((row == SUB - 1) | (row == half - 1), 0.0, pltpu.roll(u, SUB - 1, axis=0))
+    return up + down
+
+
+def in_parts(x):
+    high = x.astype(jnp.bfloat16)
+    rest = x - high.astype(jnp.float32)
+    middle = rest.astype(jnp.bfloat16)
+    low = (rest - middle.astype(jnp.float32)).astype(jnp.bfloat16)
+    return high, middle, low
 
 
 def fetch(pairs, sems):
@@ -133,9 +141,10 @@
     sems,
 ):
     pairs = [(owner_hbm, owner_ref), (offset_hbm, offset_ref), (weight_hbm, weight_ref)]
-    pairs += edge_pairs(sz, state_hbm, source_hbm, visc_hbm, u_both, q_both, v_both)
+    lists_in = fetch(pairs, sems.at[pl.ds(0, 3)])
+    pairs = edge_pairs(sz, state_hbm, source_hbm, visc_hbm, u_both, q_both, v_both)
     pairs += [(adv_hbm, adv_ref), (coup_hbm, coup_ref)]
-    arrived = fetch(pairs, sems)
+    edges_in = fetch(pairs, sems.at[pl.ds(3, 8)])
     out_ref[sz.terms : sz.first, :] = jnp.zeros((sz.first - sz.terms, LANES), jnp.float32)
     order = lax.broadcasted_iota(jnp.int32, (1, LANES), 1)
     harmonic = jnp.where(order > HARM, order - HARM, order).astype(jnp.float32)
@@ -155,13 +164,7 @@
         jnp.int32, (sz.width, sz.width), 1
     )
     before = before.astype(jnp.bfloat16)
-    arrived()
-    for c in range(sz.fields):
-        put(out_ref, sz.top(0, c), u_both[1, c, SUB - 1 : SUB, :])
-        put(out_ref, sz.bottom(0, c), u_both[0, c, 0:1, :])
-    for n, (end, at) in enumerate(((1, SUB - 1), (1, SUB - 2), (0, 0), (0, 1))):
-        put(out_ref, sz.visc + n * sz.groups, PSEUDO * v_both[end, at : at + 1, :])
-
+    lists_in()
     owner, offset, weight = owner_ref[...], offset_ref[...], weight_ref[...]
     member = lax.broadcasted_iota(jnp.int32, (sz.blocks, sz.width), 0) == owner
     member = member.astype(jnp.bfloat16)
@@ -170,27 +173,38 @@
     rank = rank.astype(jnp.int32)
     slot = owner * sz.cap + rank
     put(out_ref, sz.slot, slot.astype(jnp.float32))
-    place = (lax.broadcasted_iota(jnp.int32, (LANES, sz.width), 0) == slot % LANES).astype(jnp.float32)
+    place = (lax.broadcasted_iota(jnp.int32, (LANES, sz.width), 0) == slot % LANES).astype(jnp.bfloat16)
     held = lax.broadcasted_iota(jnp.int32, (SUB, sz.width), 0) == slot // LANES
     values = jnp.concatenate(
         [jnp.where(held, offset.astype(jnp.float32), 0.0), jnp.where(held, weight, 0.0)], axis=0
     )
-    out_ref[sz.offsets : sz.offsets + 2 * SUB, :] = lax.dot_general(
-        values, place, (((1,), (1,)), ((), ())), precision=EXACT, preferred_element_type=jnp.float32
+    parts = jnp.concatenate(in_parts(values), axis=0)
+    high, middle, low = jnp.split(
+        lax.dot_general(parts, place, (((1,), (1,)), ((), ())), preferred_element_type=jnp.float32), 3, axis=0
     )
-
+    out_ref[sz.offsets : sz.offsets + 2 * SUB, :] = high + (middle + low)
+
+    edges_in()
+    for c in range(sz.fields):
+        put(out_ref, sz.top(0, c), u_both[1, c, SUB - 1 : SUB, :])
+        put(out_ref, sz.bottom(0, c), u_both[0, c, 0:1, :])
+    for n, (end, at) in enumerate(((1, SUB - 1), (1, SUB - 2), (0, 0), (0, 1))):
+        put(out_ref, sz.visc + n * sz.groups, PSEUDO * v_both[end, at : at + 1, :])
     own, speed = matrix_of(sz, adv_ref, coup_ref)
-    for end in range(2):
-        at_low = end == 0
-        face = 0 if at_low else SUB - 1
-        visc = PSEUDO * v_both[end]
-        u = [u_both[end, c] for c in range(sz.fields)]
-        for k in range(1, ITERS):
-            u = advance(
-                sz, own, speed, u, visc, lambda c: edge_column(u[c], 0.0, at_low), lambda c: PSEUDO * q_both[end, c]
-            )
-            for c in range(sz.fields):
-                put(out_ref, sz.first + (sz.bottom if at_low else sz.top)(k, c), u[c][face : face + 1])
+    half = SUB // 2
+    row = lax.broadcasted_iota(jnp.int32, (SUB, sz.width), 0)
+
+    def both(low, high):
+        return jnp.where(row < half, low, high)
+
+    visc = PSEUDO * both(v_both[0], v_both[1])
+    source = [PSEUDO * both(q_both[0, c], q_both[1, c]) for c in range(sz.fields)]
+    u = [both(u_both[0, c], u_both[1, c]) for c in range(sz.fields)]
+    for k in range(1, ITERS):
+        u = advance(sz, own, speed, u, visc, lambda c: inside_column(u[c]), lambda c: source[c])
+        for c in range(sz.fields):
+            put(out_ref, sz.first + sz.top(k, c), u[c][SUB - 1 : SUB])
+            put(out_ref, sz.first + sz.bottom(k, c), u[c][0:1])
 
 
 def interior_kernel(
@@ -248,12 +262,11 @@
 
 
 def keep_faces(sz, b, c, top, bottom, top_ref, next_ref, bottom_ref):
-    rows = pl.ds(b * SUB + c, SUB, stride=sz.packs * SUB)
     after = pltpu.roll(top, sz.width - 1, axis=1)
     for g in range(sz.groups):
         cells = slice(g * LANES, (g + 1) * LANES)
-        top_ref.reshape(sz.groups, sz.blocks * SUB, LANES)[g, rows, :] = top[:, cells]
-        next_ref.reshape(sz.groups, sz.blocks * SUB, LANES)[g, rows, :] = after[:, cells]
+        top_ref[b, g, c] = top[:, cells]
+        next_ref[b, g, c] = after[:, cells]
     bottom_ref[c, b * SUB : (b + 1) * SUB, :] = bottom
 
 
@@ -261,7 +274,8 @@
     fields, groups = sz.fields, sz.groups
     unroll = min(sz.blocks, 16)
 
-    def first_stage(o, carry):
+    def first_stage(sub, b, carry):
+        o = sz.packs * sub + b
         offset, weight = slot_offset[o], slot_weight[o]
         at, part = offset % LANES, offset // LANES
         for c in range(fields):
@@ -269,14 +283,15 @@
             for ref in (top_ref, next_ref):
                 value = None
                 for g in range(groups):
-                    source = jnp.broadcast_to(ref[g, o, c : c + 1, :], (SUB, LANES))
+                    source = jnp.broadcast_to(ref[b, g, c, sub : sub + 1, :], (SUB, LANES))
                     taken = jnp.take_along_axis(source, at, axis=1)
                     value = taken if value is None else jnp.where(part == g, taken, value)
                 pair.append(value)
             slot_value[o, c] = weight * pair[0] + (1.0 - weight) * pair[1]
         return carry
 
-    lax.fori_loop(0, sz.blocks, first_stage, 0, unroll=unroll)
+    for sub in range(SUB):
+        lax.fori_loop(0, sz.packs, functools.partial(first_stage, sub), 0, unroll=min(sz.packs, 2))
     for b in range(sz.packs):
         for g in range(groups):
             cells = slice(g * LANES, (g + 1) * LANES)
@@ -312,9 +327,8 @@
         for ref in (top_ref, next_ref):
             value = jnp.zeros((SUB, LANES), jnp.float32)
             for b in range(packs):
-                rows = pl.ds(b * SUB + c, SUB, stride=packs * SUB)
                 for g in range(groups):
-                    source = ref.reshape(groups, sz.blocks * SUB, LANES)[g, rows, :]
+                    source = ref[b, g, c]
                     here = (part == g) & (lane // sz.cap == b)
                     value = jnp.where(here, jnp.take_along_axis(source, at, axis=1), value)
             pair.append(value)
@@ -328,7 +342,14 @@
 
 
 def mixed(kernel, bottom_ref, fields):
-    return [jnp.dot(kernel, bottom_ref[c], precision=EXACT, preferred_element_type=jnp.float32) for c in range(fields)]
+    high, middle, low = in_parts(kernel)
+    left = jnp.concatenate([high, high, high, middle, middle, low], axis=1)
+    out = []
+    for c in range(fields):
+        high, middle, low = in_parts(bottom_ref[c])
+        right = jnp.concatenate([high, middle, low, high, middle, high], axis=0)
+        out.append(jnp.dot(left, right, preferred_element_type=jnp.float32))
+    return out
 
 
 def couple_first(
@@ -464,9 +485,7 @@
         ghost = ghosts_only(lower, [upper[c][0:1] for c in range(fields)])
 
         def around(c):
-            up = jnp.where((row == 0) | (row == half), 0.0, pltpu.roll(forced[c], 1, axis=0))
-            down = jnp.where((row == SUB - 1) | (row == half - 1), 0.0, pltpu.roll(forced[c], SUB - 1, axis=0))
-            return up + down + ghost[c]
+            return inside_column(forced[c]) + ghost[c]
 
         forced = advance(sz, own, speed, forced, visc, around, None)
     for c in range(fields):
@@ -556,8 +575,8 @@
     even, odd = spread(table, blocks, interior)
     work = [
         pltpu.VMEM((blocks, fields, SUB, LANES), f32),
-        pltpu.VMEM((sz.groups, blocks, SUB, LANES), f32),
-        pltpu.VMEM((sz.groups, blocks, SUB, LANES), f32),
+        pltpu.VMEM((sz.packs, sz.groups, fields, SUB, LANES), f32),
+        pltpu.VMEM((sz.packs, sz.groups, fields, SUB, LANES), f32),
         pltpu.VMEM((sz.packs, fields, SUB, width), f32),
         pltpu.VMEM((fields, blocks, width), f32),
     ]

time: 33.6 us -> 32.6 us (0.970)
  Pallas kernels: 14 us -> 13.1 us
    pallas_call x1, Pallas kernels: 7.52 us -> 6.91 us  [per_device(): pl.pallas_call(functools.partial(couple_kernel, sz), out_shape=block, in_...]
    pallas_call x1, Pallas kernels: 2 us -> 1.66 us  [per_device(): pl.pallas_call(functools.partial(table_kernel, sz), out_shape=jax.ShapeDt...]
  transfers between devices with their start and end apart: 8 -> 8, of which waited for: 6 -> 6; matrix products, arithmetic and copies ran while one was open for 0% -> 0% of each run, Pallas kernels for 13% -> 14%
where the time goes in v4:
time: 32.6 us; the launch traced here: 32.5 us
  Pallas kernels  13.1 us (40%)
  starting transfers between devices  9.59 us (29%)
  waiting for transfers between devices  8.99 us (28%)
  between operations  0.73 us (2%)
    ppermute x8, starting transfers between devices, swap(): return lax.ppermute(piece, 'blk', [(i, i ^ mask) for i in range(blocks)])  9.59 us
    ppermute x8, waiting for transfers between devices, swap(): return lax.ppermute(piece, 'blk', [(i, i ^ mask) for i in range(blocks)])  8.99 us
    pallas_call x1, Pallas kernels, per_device(): pl.pallas_call(functools.partial(couple_kernel, sz), out_shape=block, in_...  6.91 us
    pallas_call x1, Pallas kernels, interior(): pl.pallas_call(functools.partial(interior_kernel, sz), out_shape=[block,...  4.51 us
    pallas_call x1, Pallas kernels, per_device(): pl.pallas_call(functools.partial(table_kernel, sz), out_shape=jax.ShapeDt...  1.66 us
  transfers between devices with their start and end apart: 8, of which 6 were waited for; matrix products, arithmetic and copies ran while one was open for 0% of the time, Pallas kernels for 14%

profile of v4, /device:TPU:0, one launch (start us, length us, event | category | flops | bytes accessed | tf_op | source)
XLA Modules:
  0.0 32.5 jit_solution(14754197985288706677)
XLA Ops:
  0.7 1.7 %shard_map.91 = f32[200,128]{1,0:T(8,128)S(1)} custom-call(s32[1]{0:T(128)S(6)} %copy.21.phase_ref, f32[5]{0:T(128)} %adv_hbm.5, f32[5,5]{1,0:T(8,128)} %coup_hbm.5, f32[5,64,512]{2,1,0:T(8,128)} %state_hbm.3, f32[5,64,512]{2,1,0:T(8,128)} %source_hbm.3, f32[64,512]{1,0:T(8,128)} %visc_hbm.5, s32[1,512]{1,0:T(1,128)} %bitcast.4, s32[1,512]{1,0:T(1,128)} %bitcast.5, ...), custom_call_target="tpu_custom_call" | custom-call | tf_op jit(solution)/shard_map/pallas_call | solution.py:542
  2.3 3.0 %collective-permute-start = (f32[200,128]{1,0:T(8,128)S(1)}, f32[200,128]{1,0:T(8,128)S(1)}, u32[]{:S(2)}, u32[]{:S(2)}) collective-permute-start(f32[200,128]{1,0:T(8,128)S(1)} %shard_map.91), channel_id=1, source_target_pairs={{0,2},{1,3},{2,0},{3,1},{4,6},{5,7},{6,4},{7,5},{8,10},{9,11},{10,... | collective-permute-start | bytes 307208 | tf_op jit(solution)/shard_map/ppermute | solution.py:499
  5.4 1.6 %collective-permute-start.1 = (f32[200,128]{1,0:T(8,128)S(1)}, f32[200,128]{1,0:T(8,128)S(1)}, u32[]{:S(2)}, u32[]{:S(2)}) collective-permute-start(f32[200,128]{1,0:T(8,128)S(1)} %shard_map.91), channel_id=1, source_target_pairs={{0,4},{1,5},{2,6},{3,7},{4,0},{5,1},{6,2},{7,3},{8,12},{9,13},{10,... | collective-permute-start | bytes 307208 | tf_op jit(solution)/shard_map/ppermute | solution.py:499
  6.9 2.6 %collective-permute-start.3 = (f32[200,128]{1,0:T(8,128)S(1)}, f32[200,128]{1,0:T(8,128)S(1)}, u32[]{:S(2)}, u32[]{:S(2)}) collective-permute-start(f32[200,128]{1,0:T(8,128)S(1)} %shard_map.91), channel_id=1, source_target_pairs={{0,8},{1,9},{2,10},{3,11},{4,12},{5,13},{6,14},{7,15},{8,0},{9,1},... | collective-permute-start | bytes 307208 | tf_op jit(solution)/shard_map/ppermute | solution.py:499
  9.5 0.2 collective-permute-start.5
  9.8 1.3 %collective-permute-done.1.after = f32[200,128]{1,0:T(8,128)S(1)} collective-permute-done((f32[200,128]{1,0:T(8,128)S(1)}, f32[200,128]{1,0:T(8,128)S(1)}, u32[]{:S(2)}, u32[]{:S(2)}) %collective-permute-start.1) | collective-permute-done | bytes 102432 | tf_op jit(solution)/shard_map/ppermute | solution.py:499
  11.0 4.5 %shard_map.92 = (f32[5,64,512]{2,1,0:T(8,128)}, f32[200,128]{1,0:T(8,128)S(1)}) custom-call(f32[5]{0:T(128)} %adv_hbm.5, f32[5,5]{1,0:T(8,128)} %coup_hbm.5, f32[5,64,512]{2,1,0:T(8,128)} %state_hbm.3, f32[5,64,512]{2,1,0:T(8,128)} %source_hbm.3, f32[64,512]{1,0:T(8,128)} %visc_hbm.5, ...), custom_call_target="tpu_custom_call", output_to_operand_aliasing={{1}: (5, {})} | custom-call | tf_op jit(solution)/shard_map/pallas_call | solution.py:556
  15.6 0.1 collective-permute-start.2
  15.6 1.7 %collective-permute-done.3 = f32[200,128]{1,0:T(8,128)S(1)} collective-permute-done((f32[200,128]{1,0:T(8,128)S(1)}, f32[200,128]{1,0:T(8,128)S(1)}, u32[]{:S(2)}, u32[]{:S(2)}) %collective-permute-start.3) | collective-permute-done | bytes 102432 | tf_op jit(solution)/shard_map/ppermute | solution.py:499
  17.4 0.5 %collective-permute-start.4 = (f32[200,128]{1,0:T(8,128)S(1)}, f32[200,128]{1,0:T(8,128)S(1)}, u32[]{:S(2)}, u32[]{:S(2)}) collective-permute-start(f32[200,128]{1,0:T(8,128)S(1)} %collective-permute-done.3), channel_id=1, source_target_pairs={{0,2},{1,3},{2,0},{3,1},{4,6},{5,7},{6,4},{7,5},{8,10},{9,11},{10,... | collective-permute-start | bytes 307208 | tf_op jit(solution)/shard_map/ppermute | solution.py:499
  17.9 0.0 collective-permute-done.5
  17.9 1.5 %collective-permute-start.6 = (f32[200,128]{1,0:T(8,128)S(1)}, f32[200,128]{1,0:T(8,128)S(1)}, u32[]{:S(2)}, u32[]{:S(2)}) collective-permute-start(f32[200,128]{1,0:T(8,128)S(1)} %collective-permute-done.5), channel_id=1, source_target_pairs={{0,2},{1,3},{2,0},{3,1},{4,6},{5,7},{6,4},{7,5},{8,10},{9,11},{10,... | collective-permute-start | bytes 307208 | tf_op jit(solution)/shard_map/ppermute | solution.py:499
  19.4 0.0 collective-permute-done
  19.4 0.8 %collective-permute-done.2 = f32[200,128]{1,0:T(8,128)S(1)} collective-permute-done((f32[200,128]{1,0:T(8,128)S(1)}, f32[200,128]{1,0:T(8,128)S(1)}, u32[]{:S(2)}, u32[]{:S(2)}) %collective-permute-start.2) | collective-permute-done | bytes 102432 | tf_op jit(solution)/shard_map/ppermute | solution.py:499
  20.3 1.7 %collective-permute-done.4 = f32[200,128]{1,0:T(8,128)S(1)} collective-permute-done((f32[200,128]{1,0:T(8,128)S(1)}, f32[200,128]{1,0:T(8,128)S(1)}, u32[]{:S(2)}, u32[]{:S(2)}) %collective-permute-start.4) | collective-permute-done | bytes 102432 | tf_op jit(solution)/shard_map/ppermute | solution.py:499
  22.1 1.1 %collective-permute-done.6 = f32[200,128]{1,0:T(8,128)S(1)} collective-permute-done((f32[200,128]{1,0:T(8,128)S(1)}, f32[200,128]{1,0:T(8,128)S(1)}, u32[]{:S(2)}, u32[]{:S(2)}) %collective-permute-start.6) | collective-permute-done | bytes 102432 | tf_op jit(solution)/shard_map/ppermute | solution.py:499
  23.2 0.1 collective-permute-start.7
  23.2 2.3 %collective-permute-done.7.odd_ref = f32[1600,128]{1,0:T(8,128)S(1)} collective-permute-done((f32[1600,128]{1,0:T(8,128)S(1)}, f32[1600,128]{1,0:T(8,128)S(1)}, u32[]{:S(2)}, u32[]{:S(2)}) %collective-permute-start.7) | collective-permute-done | bytes 819232 | tf_op jit(solution)/shard_map/ppermute | solution.py:499
  25.5 6.9 %shard_map.93 = f32[5,64,512]{2,1,0:T(8,128)} custom-call(s32[1]{0:T(128)} %bitcast.me_ref, f32[5]{0:T(128)} %adv_hbm.5, f32[5,5]{1,0:T(8,128)} %coup_hbm.5, f32[64,512]{1,0:T(8,128)} %visc_hbm.5, f32[1600,128]{1,0:T(8,128)S(1)} %constant_dynamic-update-slice_fusion.even_ref, ...), custom_call_target="tpu_custom_call", output_to_operand_aliasing={{}: (6, {})} | custom-call | tf_op jit(solution)/shard_map/pallas_call | solution.py:595
  (8 shorter events, 0.1 us)
Async XLA Ops:
  2.3 17.1 %collective-permute-start = (f32[200,128]{1,0:T(8,128)S(1)}, f32[200,128]{1,0:T(8,128)S(1)}, u32[]{:S(2)}, u32[]{:S(2)}) collective-permute-start(f32[200,128]{1,0:T(8,128)S(1)} %shard_map.91), channel_id=1, source_target_pairs={{0,2},{1,3},{2,0},{3,1},{4,6},{5,7},{6,4},{7,5},{8,10},{9,11},{10,... | collective-permute-start | bytes 307208 | tf_op jit(solution)/shard_map/ppermute | solution.py:499
  5.4 5.7 %collective-permute-start.1 = (f32[200,128]{1,0:T(8,128)S(1)}, f32[200,128]{1,0:T(8,128)S(1)}, u32[]{:S(2)}, u32[]{:S(2)}) collective-permute-start(f32[200,128]{1,0:T(8,128)S(1)} %shard_map.91), channel_id=1, source_target_pairs={{0,4},{1,5},{2,6},{3,7},{4,0},{5,1},{6,2},{7,3},{8,12},{9,13},{10,... | collective-permute-start | bytes 307208 | tf_op jit(solution)/shard_map/ppermute | solution.py:499
  6.9 10.4 %collective-permute-start.3 = (f32[200,128]{1,0:T(8,128)S(1)}, f32[200,128]{1,0:T(8,128)S(1)}, u32[]{:S(2)}, u32[]{:S(2)}) collective-permute-start(f32[200,128]{1,0:T(8,128)S(1)} %shard_map.91), channel_id=1, source_target_pairs={{0,8},{1,9},{2,10},{3,11},{4,12},{5,13},{6,14},{7,15},{8,0},{9,1},... | collective-permute-start | bytes 307208 | tf_op jit(solution)/shard_map/ppermute | solution.py:499
  9.5 8.4 %collective-permute-start.5 = (f32[200,128]{1,0:T(8,128)S(1)}, f32[200,128]{1,0:T(8,128)S(1)}, u32[]{:S(2)}, u32[]{:S(2)}) collective-permute-start(f32[200,128]{1,0:T(8,128)S(1)} %shard_map.91), channel_id=1, source_target_pairs={{0,12},{1,13},{2,14},{3,15},{4,8},{5,9},{6,10},{7,11},{8,4},{9,5},... | collective-permute-start | bytes 307208 | tf_op jit(solution)/shard_map/ppermute | solution.py:499
  15.6 4.7 %collective-permute-start.2 = (f32[200,128]{1,0:T(8,128)S(1)}, f32[200,128]{1,0:T(8,128)S(1)}, u32[]{:S(2)}, u32[]{:S(2)}) collective-permute-start(f32[200,128]{1,0:T(8,128)S(1)} %get-tuple-element.7), channel_id=1, source_target_pairs={{0,2},{1,3},{2,0},{3,1},{4,6},{5,7},{6,4},{7,5},{8,10},{9,11},{10,... | collective-permute-start | bytes 307208 | tf_op jit(solution)/shard_map/ppermute | solution.py:499
  17.4 4.7 %collective-permute-start.4 = (f32[200,128]{1,0:T(8,128)S(1)}, f32[200,128]{1,0:T(8,128)S(1)}, u32[]{:S(2)}, u32[]{:S(2)}) collective-permute-start(f32[200,128]{1,0:T(8,128)S(1)} %collective-permute-done.3), channel_id=1, source_target_pairs={{0,2},{1,3},{2,0},{3,1},{4,6},{5,7},{6,4},{7,5},{8,10},{9,11},{10,... | collective-permute-start | bytes 307208 | tf_op jit(solution)/shard_map/ppermute | solution.py:499
  17.9 5.2 %collective-permute-start.6 = (f32[200,128]{1,0:T(8,128)S(1)}, f32[200,128]{1,0:T(8,128)S(1)}, u32[]{:S(2)}, u32[]{:S(2)}) collective-permute-start(f32[200,128]{1,0:T(8,128)S(1)} %collective-permute-done.5), channel_id=1, source_target_pairs={{0,2},{1,3},{2,0},{3,1},{4,6},{5,7},{6,4},{7,5},{8,10},{9,11},{10,... | collective-permute-start | bytes 307208 | tf_op jit(solution)/shard_map/ppermute | solution.py:499
  23.2 2.4 %collective-permute-start.7 = (f32[1600,128]{1,0:T(8,128)S(1)}, f32[1600,128]{1,0:T(8,128)S(1)}, u32[]{:S(2)}, u32[]{:S(2)}) collective-permute-start(f32[1600,128]{1,0:T(8,128)S(1)} %constant_dynamic-update-slice_fusion.even_ref), channel_id=1, source_target_pairs={{0,1},{1,0},{2,3},{3,2},{4,5},{5,4},{6,7},{7,6},{8,9},{9,8},{10,11... | collective-permute-start | bytes 2457608 | tf_op jit(solution)/shard_map/ppermute | solution.py:499

commit v5 on v4

--- a/solution.py
+++ b/solution.py
@@ -270,10 +270,8 @@
     bottom_ref[c, b * SUB : (b + 1) * SUB, :] = bottom
 
 
-def gather(sz, slot_offset, slot_weight, slot_value, top_ref, next_ref, taker_ref, place_ref, lower_ref):
+def gather(sz, slot_offset, slot_weight, slot_value, owner_value, top_ref, next_ref, taker_ref, place_ref, lower_ref):
     fields, groups = sz.fields, sz.groups
-    unroll = min(sz.blocks, 16)
-
     def first_stage(sub, b, carry):
         o = sz.packs * sub + b
         offset, weight = slot_offset[o], slot_weight[o]
@@ -292,20 +290,35 @@
 
     for sub in range(SUB):
         lax.fori_loop(0, sz.packs, functools.partial(first_stage, sub), 0, unroll=min(sz.packs, 2))
+    lane = lax.broadcasted_iota(jnp.int32, (SUB, LANES), 1)
+    for m in range(SUB):
+
+        def regroup(b, carry):
+            for c in range(fields):
+                tile = None
+                for n in range(sz.packs):
+                    value = slot_value[m * sz.packs + n, c]
+                    if not isinstance(b, int) or b != n:
+                        value = pltpu.roll(value, (n - b) * sz.cap % LANES, axis=1)
+                    tile = value if tile is None else jnp.where(lane // sz.cap == n, value, tile)
+                owner_value[b, m, c] = tile
+            return carry
+
+        if sz.packs <= 4:
+            for b in range(sz.packs):
+                regroup(b, 0)
+        else:
+            lax.fori_loop(0, sz.packs, regroup, 0)
     for b in range(sz.packs):
         for g in range(groups):
             cells = slice(g * LANES, (g + 1) * LANES)
             taker, place = taker_ref[b, :, cells], place_ref[b, :, cells]
-
-            def second_stage(o, found):
-                mine = taker == o
-                return tuple(
-                    jnp.where(mine, jnp.take_along_axis(slot_value[o, c], place, axis=1), found[c])
-                    for c in range(fields)
-                )
-
-            zero = jnp.zeros((SUB, LANES), jnp.float32)
-            found = lax.fori_loop(0, sz.blocks, second_stage, (zero,) * fields, unroll=unroll)
+            found = [jnp.zeros((SUB, LANES), jnp.float32)] * fields
+            for m in range(SUB):
+                mine = taker == m
+                for c in range(fields):
+                    taken = jnp.take_along_axis(owner_value[b, m, c], place, axis=1)
+                    found[c] = jnp.where(mine, taken, found[c])
             for c in range(fields):
                 lower_ref[b, c, :, cells] = found[c]
 
@@ -320,7 +333,6 @@
         return jnp.concatenate(parts + [parts[0]] * (SUB - groups), axis=0)
 
     taker, place = stacked(taker), stacked(place)
-    place = place + taker % packs * sz.cap
     ghost = []
     for c in range(fields):
         pair = []
@@ -336,7 +348,7 @@
         found = jnp.zeros((SUB, LANES), jnp.float32)
         for m in range(SUB):
             source = jnp.broadcast_to(held[m : m + 1], (SUB, LANES))
-            found = jnp.where(taker // packs == m, jnp.take_along_axis(source, place, axis=1), found)
+            found = jnp.where(taker == m, jnp.take_along_axis(source, place, axis=1), found)
         ghost.append(jnp.concatenate([found[g : g + 1] for g in range(groups)], axis=1))
     return ghost
 
@@ -368,6 +380,7 @@
     outer_ref,
     ghost_ref,
     slot_value,
+    owner_value,
     top_ref,
     next_ref,
     lower_ref,
@@ -397,8 +410,9 @@
             slot_weight[o] = tile_w
     for b in range(packs):
         slots = wide(b, sz.slot).astype(jnp.int32)
-        taker_ref[b] = jnp.bitwise_xor(slots // sz.cap, me)
-        place_ref[b] = slots % sz.cap + b * sz.cap
+        owner = jnp.bitwise_xor(slots // sz.cap, me)
+        taker_ref[b] = owner // packs
+        place_ref[b] = owner % packs * sz.cap + slots % sz.cap
         for n in range(4):
             visc_ref[n, b] = wide(b, sz.visc + n * groups)
     basis = jnp.concatenate([line(b, sz.basis) for b in range(packs)], axis=0)
@@ -419,7 +433,7 @@
         out[...] = tile
 
     upper = mixed(kernel, bottom_ref, fields)
-    gather(sz, slot_offset, slot_weight, slot_value, top_ref, next_ref, taker_ref, place_ref, lower_ref)
+    gather(sz, slot_offset, slot_weight, slot_value, owner_value, top_ref, next_ref, taker_ref, place_ref, lower_ref)
     for c in range(fields):
         ghost_ref[0, c] = lower_ref[0, c]
         ghost_ref[1, c] = upper[c][0:SUB]
@@ -430,9 +444,9 @@
 
 def couple_kernel(sz, me_ref, adv_hbm, coup_hbm, visc_hbm, even_ref, odd_ref, inside_hbm, out_hbm, *scratch):
     adv_ref, coup_ref, ends_ref, edge_ref, sems = scratch[:5]
-    carried, work = scratch[5:-5], scratch[-5:]
+    carried, work = scratch[5:-6], scratch[-6:]
     slot_offset, slot_weight, own_offset, own_weight, taker_ref, place_ref, kernel_ref, visc_ref, outer_ref, ghost_ref = carried
-    slot_value, top_ref, next_ref, lower_ref, bottom_ref = work
+    slot_value, owner_value, top_ref, next_ref, lower_ref, bottom_ref = work
     ends = [pl.ds(0, SUB), pl.ds(sz.rows - SUB, SUB)]
     pairs = [(adv_hbm, adv_ref), (coup_hbm, coup_ref)]
     pairs += [(visc_hbm.at[here, :], ends_ref.at[n]) for n, here in enumerate(ends)]
@@ -463,7 +477,7 @@
             lower = gather_own(sz, own_offset[...], own_weight[...], top_ref, next_ref, taker, place)
         else:
             upper = mixed(kernel, bottom_ref, fields)
-            gather(sz, slot_offset, slot_weight, slot_value, top_ref, next_ref, taker_ref, place_ref, lower_ref)
+            gather(sz, slot_offset, slot_weight, slot_value, owner_value, top_ref, next_ref, taker_ref, place_ref, lower_ref)
             lower = [lower_ref[0, c, 0:1, :] for c in range(fields)]
             if k == 1:
                 arrived()
@@ -575,6 +589,7 @@
     even, odd = spread(table, blocks, interior)
     work = [
         pltpu.VMEM((blocks, fields, SUB, LANES), f32),
+        pltpu.VMEM((sz.packs, SUB, fields, SUB, LANES), f32),
         pltpu.VMEM((sz.packs, sz.groups, fields, SUB, LANES), f32),
         pltpu.VMEM((sz.packs, sz.groups, fields, SUB, LANES), f32),
         pltpu.VMEM((sz.packs, fields, SUB, width), f32),

time: 32.6 us -> 32 us (0.982)
  Pallas kernels: 13.1 us -> 12.4 us
    pallas_call x1, Pallas kernels: 6.91 us -> 6.22 us  [per_device(): pl.pallas_call(functools.partial(couple_kernel, sz), out_shape=block, in_...]
where the time goes in v5:
time: 32 us; the launch traced here: 31.8 us
  Pallas kernels  12.4 us (39%)
  starting transfers between devices  9.59 us (30%)
  waiting for transfers between devices  8.99 us (28%)
  between operations  0.73 us (2%)
    ppermute x8, starting transfers between devices, swap(): return lax.ppermute(piece, 'blk', [(i, i ^ mask) for i in range(blocks)])  9.59 us
    ppermute x8, waiting for transfers between devices, swap(): return lax.ppermute(piece, 'blk', [(i, i ^ mask) for i in range(blocks)])  8.99 us
    pallas_call x1, Pallas kernels, per_device(): pl.pallas_call(functools.partial(couple_kernel, sz), out_shape=block, in_...  6.22 us
    pallas_call x1, Pallas kernels, interior(): pl.pallas_call(functools.partial(interior_kernel, sz), out_shape=[block,...  4.51 us
    pallas_call x1, Pallas kernels, per_device(): pl.pallas_call(functools.partial(table_kernel, sz), out_shape=jax.ShapeDt...  1.66 us
  transfers between devices with their start and end apart: 8, of which 6 were waited for; matrix products, arithmetic and copies ran while one was open for 0% of the time, Pallas kernels for 14%

profile of v5, /device:TPU:0, one launch (start us, length us, event | category | flops | bytes accessed | tf_op | source)
XLA Modules:
  0.0 31.8 jit_solution(9797076507528528319)
XLA Ops:
  0.7 1.7 %shard_map.91 = f32[200,128]{1,0:T(8,128)S(1)} custom-call(s32[1]{0:T(128)S(6)} %copy.21.phase_ref, f32[5]{0:T(128)} %adv_hbm.5, f32[5,5]{1,0:T(8,128)} %coup_hbm.5, f32[5,64,512]{2,1,0:T(8,128)} %state_hbm.3, f32[5,64,512]{2,1,0:T(8,128)} %source_hbm.3, f32[64,512]{1,0:T(8,128)} %visc_hbm.5, s32[1,512]{1,0:T(1,128)} %bitcast.4, s32[1,512]{1,0:T(1,128)} %bitcast.5, ...), custom_call_target="tpu_custom_call" | custom-call | tf_op jit(solution)/shard_map/pallas_call | solution.py:556
  2.3 3.0 %collective-permute-start = (f32[200,128]{1,0:T(8,128)S(1)}, f32[200,128]{1,0:T(8,128)S(1)}, u32[]{:S(2)}, u32[]{:S(2)}) collective-permute-start(f32[200,128]{1,0:T(8,128)S(1)} %shard_map.91), channel_id=1, source_target_pairs={{0,2},{1,3},{2,0},{3,1},{4,6},{5,7},{6,4},{7,5},{8,10},{9,11},{10,... | collective-permute-start | bytes 307208 | tf_op jit(solution)/shard_map/ppermute | solution.py:513
  5.4 1.6 %collective-permute-start.1 = (f32[200,128]{1,0:T(8,128)S(1)}, f32[200,128]{1,0:T(8,128)S(1)}, u32[]{:S(2)}, u32[]{:S(2)}) collective-permute-start(f32[200,128]{1,0:T(8,128)S(1)} %shard_map.91), channel_id=1, source_target_pairs={{0,4},{1,5},{2,6},{3,7},{4,0},{5,1},{6,2},{7,3},{8,12},{9,13},{10,... | collective-permute-start | bytes 307208 | tf_op jit(solution)/shard_map/ppermute | solution.py:513
  6.9 2.6 %collective-permute-start.3 = (f32[200,128]{1,0:T(8,128)S(1)}, f32[200,128]{1,0:T(8,128)S(1)}, u32[]{:S(2)}, u32[]{:S(2)}) collective-permute-start(f32[200,128]{1,0:T(8,128)S(1)} %shard_map.91), channel_id=1, source_target_pairs={{0,8},{1,9},{2,10},{3,11},{4,12},{5,13},{6,14},{7,15},{8,0},{9,1},... | collective-permute-start | bytes 307208 | tf_op jit(solution)/shard_map/ppermute | solution.py:513
  9.5 0.2 collective-permute-start.5
  9.8 1.3 %collective-permute-done.1.after = f32[200,128]{1,0:T(8,128)S(1)} collective-permute-done((f32[200,128]{1,0:T(8,128)S(1)}, f32[200,128]{1,0:T(8,128)S(1)}, u32[]{:S(2)}, u32[]{:S(2)}) %collective-permute-start.1) | collective-permute-done | bytes 102432 | tf_op jit(solution)/shard_map/ppermute | solution.py:513
  11.0 4.5 %shard_map.92 = (f32[5,64,512]{2,1,0:T(8,128)}, f32[200,128]{1,0:T(8,128)S(1)}) custom-call(f32[5]{0:T(128)} %adv_hbm.5, f32[5,5]{1,0:T(8,128)} %coup_hbm.5, f32[5,64,512]{2,1,0:T(8,128)} %state_hbm.3, f32[5,64,512]{2,1,0:T(8,128)} %source_hbm.3, f32[64,512]{1,0:T(8,128)} %visc_hbm.5, ...), custom_call_target="tpu_custom_call", output_to_operand_aliasing={{1}: (5, {})} | custom-call | tf_op jit(solution)/shard_map/pallas_call | solution.py:570
  15.6 0.1 collective-permute-start.2
  15.6 1.7 %collective-permute-done.3 = f32[200,128]{1,0:T(8,128)S(1)} collective-permute-done((f32[200,128]{1,0:T(8,128)S(1)}, f32[200,128]{1,0:T(8,128)S(1)}, u32[]{:S(2)}, u32[]{:S(2)}) %collective-permute-start.3) | collective-permute-done | bytes 102432 | tf_op jit(solution)/shard_map/ppermute | solution.py:513
  17.4 0.5 %collective-permute-start.4 = (f32[200,128]{1,0:T(8,128)S(1)}, f32[200,128]{1,0:T(8,128)S(1)}, u32[]{:S(2)}, u32[]{:S(2)}) collective-permute-start(f32[200,128]{1,0:T(8,128)S(1)} %collective-permute-done.3), channel_id=1, source_target_pairs={{0,2},{1,3},{2,0},{3,1},{4,6},{5,7},{6,4},{7,5},{8,10},{9,11},{10,... | collective-permute-start | bytes 307208 | tf_op jit(solution)/shard_map/ppermute | solution.py:513
  17.9 0.0 collective-permute-done.5
  17.9 1.5 %collective-permute-start.6 = (f32[200,128]{1,0:T(8,128)S(1)}, f32[200,128]{1,0:T(8,128)S(1)}, u32[]{:S(2)}, u32[]{:S(2)}) collective-permute-start(f32[200,128]{1,0:T(8,128)S(1)} %collective-permute-done.5), channel_id=1, source_target_pairs={{0,2},{1,3},{2,0},{3,1},{4,6},{5,7},{6,4},{7,5},{8,10},{9,11},{10,... | collective-permute-start | bytes 307208 | tf_op jit(solution)/shard_map/ppermute | solution.py:513
  19.4 0.0 collective-permute-done
  19.4 0.8 %collective-permute-done.2 = f32[200,128]{1,0:T(8,128)S(1)} collective-permute-done((f32[200,128]{1,0:T(8,128)S(1)}, f32[200,128]{1,0:T(8,128)S(1)}, u32[]{:S(2)}, u32[]{:S(2)}) %collective-permute-start.2) | collective-permute-done | bytes 102432 | tf_op jit(solution)/shard_map/ppermute | solution.py:513
  20.3 1.7 %collective-permute-done.4 = f32[200,128]{1,0:T(8,128)S(1)} collective-permute-done((f32[200,128]{1,0:T(8,128)S(1)}, f32[200,128]{1,0:T(8,128)S(1)}, u32[]{:S(2)}, u32[]{:S(2)}) %collective-permute-start.4) | collective-permute-done | bytes 102432 | tf_op jit(solution)/shard_map/ppermute | solution.py:513
  22.1 1.1 %collective-permute-done.6 = f32[200,128]{1,0:T(8,128)S(1)} collective-permute-done((f32[200,128]{1,0:T(8,128)S(1)}, f32[200,128]{1,0:T(8,128)S(1)}, u32[]{:S(2)}, u32[]{:S(2)}) %collective-permute-start.6) | collective-permute-done | bytes 102432 | tf_op jit(solution)/shard_map/ppermute | solution.py:513
  23.2 0.1 collective-permute-start.7
  23.2 2.3 %collective-permute-done.7.odd_ref = f32[1600,128]{1,0:T(8,128)S(1)} collective-permute-done((f32[1600,128]{1,0:T(8,128)S(1)}, f32[1600,128]{1,0:T(8,128)S(1)}, u32[]{:S(2)}, u32[]{:S(2)}) %collective-permute-start.7) | collective-permute-done | bytes 819232 | tf_op jit(solution)/shard_map/ppermute | solution.py:513
  25.5 6.2 %shard_map.93 = f32[5,64,512]{2,1,0:T(8,128)} custom-call(s32[1]{0:T(128)} %bitcast.me_ref, f32[5]{0:T(128)} %adv_hbm.5, f32[5,5]{1,0:T(8,128)} %coup_hbm.5, f32[64,512]{1,0:T(8,128)} %visc_hbm.5, f32[1600,128]{1,0:T(8,128)S(1)} %constant_dynamic-update-slice_fusion.even_ref, ...), custom_call_target="tpu_custom_call", output_to_operand_aliasing={{}: (6, {})} | custom-call | tf_op jit(solution)/shard_map/pallas_call | solution.py:610
  (8 shorter events, 0.1 us)
Async XLA Ops:
  2.3 17.1 %collective-permute-start = (f32[200,128]{1,0:T(8,128)S(1)}, f32[200,128]{1,0:T(8,128)S(1)}, u32[]{:S(2)}, u32[]{:S(2)}) collective-permute-start(f32[200,128]{1,0:T(8,128)S(1)} %shard_map.91), channel_id=1, source_target_pairs={{0,2},{1,3},{2,0},{3,1},{4,6},{5,7},{6,4},{7,5},{8,10},{9,11},{10,... | collective-permute-start | bytes 307208 | tf_op jit(solution)/shard_map/ppermute | solution.py:513
  5.4 5.7 %collective-permute-start.1 = (f32[200,128]{1,0:T(8,128)S(1)}, f32[200,128]{1,0:T(8,128)S(1)}, u32[]{:S(2)}, u32[]{:S(2)}) collective-permute-start(f32[200,128]{1,0:T(8,128)S(1)} %shard_map.91), channel_id=1, source_target_pairs={{0,4},{1,5},{2,6},{3,7},{4,0},{5,1},{6,2},{7,3},{8,12},{9,13},{10,... | collective-permute-start | bytes 307208 | tf_op jit(solution)/shard_map/ppermute | solution.py:513
  6.9 10.4 %collective-permute-start.3 = (f32[200,128]{1,0:T(8,128)S(1)}, f32[200,128]{1,0:T(8,128)S(1)}, u32[]{:S(2)}, u32[]{:S(2)}) collective-permute-start(f32[200,128]{1,0:T(8,128)S(1)} %shard_map.91), channel_id=1, source_target_pairs={{0,8},{1,9},{2,10},{3,11},{4,12},{5,13},{6,14},{7,15},{8,0},{9,1},... | collective-permute-start | bytes 307208 | tf_op jit(solution)/shard_map/ppermute | solution.py:513
  9.5 8.4 %collective-permute-start.5 = (f32[200,128]{1,0:T(8,128)S(1)}, f32[200,128]{1,0:T(8,128)S(1)}, u32[]{:S(2)}, u32[]{:S(2)}) collective-permute-start(f32[200,128]{1,0:T(8,128)S(1)} %shard_map.91), channel_id=1, source_target_pairs={{0,12},{1,13},{2,14},{3,15},{4,8},{5,9},{6,10},{7,11},{8,4},{9,5},... | collective-permute-start | bytes 307208 | tf_op jit(solution)/shard_map/ppermute | solution.py:513
  15.6 4.7 %collective-permute-start.2 = (f32[200,128]{1,0:T(8,128)S(1)}, f32[200,128]{1,0:T(8,128)S(1)}, u32[]{:S(2)}, u32[]{:S(2)}) collective-permute-start(f32[200,128]{1,0:T(8,128)S(1)} %get-tuple-element.7), channel_id=1, source_target_pairs={{0,2},{1,3},{2,0},{3,1},{4,6},{5,7},{6,4},{7,5},{8,10},{9,11},{10,... | collective-permute-start | bytes 307208 | tf_op jit(solution)/shard_map/ppermute | solution.py:513
  17.4 4.7 %collective-permute-start.4 = (f32[200,128]{1,0:T(8,128)S(1)}, f32[200,128]{1,0:T(8,128)S(1)}, u32[]{:S(2)}, u32[]{:S(2)}) collective-permute-start(f32[200,128]{1,0:T(8,128)S(1)} %collective-permute-done.3), channel_id=1, source_target_pairs={{0,2},{1,3},{2,0},{3,1},{4,6},{5,7},{6,4},{7,5},{8,10},{9,11},{10,... | collective-permute-start | bytes 307208 | tf_op jit(solution)/shard_map/ppermute | solution.py:513
  17.9 5.2 %collective-permute-start.6 = (f32[200,128]{1,0:T(8,128)S(1)}, f32[200,128]{1,0:T(8,128)S(1)}, u32[]{:S(2)}, u32[]{:S(2)}) collective-permute-start(f32[200,128]{1,0:T(8,128)S(1)} %collective-permute-done.5), channel_id=1, source_target_pairs={{0,2},{1,3},{2,0},{3,1},{4,6},{5,7},{6,4},{7,5},{8,10},{9,11},{10,... | collective-permute-start | bytes 307208 | tf_op jit(solution)/shard_map/ppermute | solution.py:513
  23.2 2.4 %collective-permute-start.7 = (f32[1600,128]{1,0:T(8,128)S(1)}, f32[1600,128]{1,0:T(8,128)S(1)}, u32[]{:S(2)}, u32[]{:S(2)}) collective-permute-start(f32[1600,128]{1,0:T(8,128)S(1)} %constant_dynamic-update-slice_fusion.even_ref), channel_id=1, source_target_pairs={{0,1},{1,0},{2,3},{3,2},{4,5},{5,4},{6,7},{7,6},{8,9},{9,8},{10,11... | collective-permute-start | bytes 2457608 | tf_op jit(solution)/shard_map/ppermute | solution.py:513

commit v6 on v5

--- a/solution.py
+++ b/solution.py
@@ -31,7 +31,7 @@
         self.weights = self.offsets + SUB
         self.terms = self.weights + SUB
         self.basis = self.terms + 1
-        self.first = -(-(self.basis + 1) // SUB) * SUB
+        self.first = -(-(self.basis + 2) // SUB) * SUB
         self.rest = -(-2 * (ITERS - 1) * faces // SUB) * SUB
 
         self.table = self.first + self.rest
@@ -508,7 +508,7 @@
     fetch([(edge_ref.at[n], out_hbm.at[:, here, :]) for n, here in enumerate(ends)], sems)()
 
 
-def spread(table, blocks, between):
+def spread(table, blocks, spare, between):
     def swap(piece, mask):
         return lax.ppermute(piece, "blk", [(i, i ^ mask) for i in range(blocks)])
 
@@ -518,8 +518,9 @@
         have = jnp.concatenate(parts, axis=0) if len(parts) > 1 else parts[0]
         parts = [have] + [swap(have, mask) for mask in masks]
         bit = bit * (len(masks) + 1)
-    parts[1] = between(parts[1])
-    twos = [swap(part, 2) for part in parts]
+    twos = [between(swap(parts[0], 2))]
+    parts[1:] = [part.at[spare].set(twos[0][spare]) for part in parts[1:]]
+    twos += [swap(part, 2) for part in parts[1:]]
     even = jnp.concatenate([t for pair in zip(parts, twos) for t in pair], axis=0)
     return even, swap(even, 1)
 
@@ -586,7 +587,7 @@
         insides.append(inside)
         return piece
 
-    even, odd = spread(table, blocks, interior)
+    even, odd = spread(table, blocks, sz.first - 1, interior)
     work = [
         pltpu.VMEM((blocks, fields, SUB, LANES), f32),
         pltpu.VMEM((sz.packs, SUB, fields, SUB, LANES), f32),

time: 32 us -> 32 us (level)
  waiting for transfers between devices: 8.99 us -> 8.55 us
  starting transfers between devices: 9.59 us -> 9.99 us
    ppermute x8, waiting for transfers between devices: 8.99 us -> 8.55 us  [swap(): return lax.ppermute(piece, 'blk', [(i, i ^ mask) for i in range(blocks)])]
    ppermute x8, starting transfers between devices: 9.59 us -> 9.99 us  [swap(): return lax.ppermute(piece, 'blk', [(i, i ^ mask) for i in range(blocks)])]
  transfers between devices with their start and end apart: 8 -> 8, of which waited for: 6 -> 5; matrix products, arithmetic and copies ran while one was open for 0% -> 0% of each run, Pallas kernels for 14% -> 14%
where the time goes in v6:
time: 32 us; the launch traced here: 31.9 us
  Pallas kernels  12.4 us (39%)
  starting transfers between devices  9.99 us (31%)
  waiting for transfers between devices  8.55 us (27%)
  between operations  0.75 us (2%)
    ppermute x8, starting transfers between devices, swap(): return lax.ppermute(piece, 'blk', [(i, i ^ mask) for i in range(blocks)])  9.99 us
    ppermute x8, waiting for transfers between devices, swap(): return lax.ppermute(piece, 'blk', [(i, i ^ mask) for i in range(blocks)])  8.55 us
    pallas_call x1, Pallas kernels, per_device(): pl.pallas_call(functools.partial(couple_kernel, sz), out_shape=block, in_...  6.22 us
    pallas_call x1, Pallas kernels, interior(): pl.pallas_call(functools.partial(interior_kernel, sz), out_shape=[block,...  4.51 us
    pallas_call x1, Pallas kernels, per_device(): pl.pallas_call(functools.partial(table_kernel, sz), out_shape=jax.ShapeDt...  1.66 us
  transfers between devices with their start and end apart: 8, of which 5 were waited for; matrix products, arithmetic and copies ran while one was open for 0% of the time, Pallas kernels for 14%

profile of v6, /device:TPU:0, one launch (start us, length us, event | category | flops | bytes accessed | tf_op | source)
XLA Modules:
  0.0 31.9 jit_solution(15846614190217782719)
XLA Ops:
  0.7 1.7 %shard_map.91 = f32[200,128]{1,0:T(8,128)S(1)} custom-call(s32[1]{0:T(128)S(6)} %copy.24.phase_ref, f32[5]{0:T(128)} %adv_hbm.5, f32[5,5]{1,0:T(8,128)} %coup_hbm.5, f32[5,64,512]{2,1,0:T(8,128)} %state_hbm.3, f32[5,64,512]{2,1,0:T(8,128)} %source_hbm.3, f32[64,512]{1,0:T(8,128)} %visc_hbm.5, s32[1,512]{1,0:T(1,128)} %bitcast.4, s32[1,512]{1,0:T(1,128)} %bitcast.5, ...), custom_call_target="tpu_custom_call" | custom-call | tf_op jit(solution)/shard_map/pallas_call | solution.py:557
  2.3 3.0 %collective-permute-start = (f32[200,128]{1,0:T(8,128)S(1)}, f32[200,128]{1,0:T(8,128)S(1)}, u32[]{:S(2)}, u32[]{:S(2)}) collective-permute-start(f32[200,128]{1,0:T(8,128)S(1)} %shard_map.91), channel_id=1, source_target_pairs={{0,2},{1,3},{2,0},{3,1},{4,6},{5,7},{6,4},{7,5},{8,10},{9,11},{10,... | collective-permute-start | bytes 307208 | tf_op jit(solution)/shard_map/ppermute | solution.py:513
  5.4 1.6 %collective-permute-start.1 = (f32[200,128]{1,0:T(8,128)S(1)}, f32[200,128]{1,0:T(8,128)S(1)}, u32[]{:S(2)}, u32[]{:S(2)}) collective-permute-start(f32[200,128]{1,0:T(8,128)S(1)} %shard_map.91), channel_id=1, source_target_pairs={{0,4},{1,5},{2,6},{3,7},{4,0},{5,1},{6,2},{7,3},{8,12},{9,13},{10,... | collective-permute-start | bytes 307208 | tf_op jit(solution)/shard_map/ppermute | solution.py:513
  6.9 2.6 %collective-permute-start.3 = (f32[200,128]{1,0:T(8,128)S(1)}, f32[200,128]{1,0:T(8,128)S(1)}, u32[]{:S(2)}, u32[]{:S(2)}) collective-permute-start(f32[200,128]{1,0:T(8,128)S(1)} %shard_map.91), channel_id=1, source_target_pairs={{0,8},{1,9},{2,10},{3,11},{4,12},{5,13},{6,14},{7,15},{8,0},{9,1},... | collective-permute-start | bytes 307208 | tf_op jit(solution)/shard_map/ppermute | solution.py:513
  9.5 0.2 collective-permute-start.5
  9.8 0.0 collective-permute-done.after
  9.8 4.5 %shard_map.92 = (f32[5,64,512]{2,1,0:T(8,128)}, f32[200,128]{1,0:T(8,128)S(1)}) custom-call(f32[5]{0:T(128)} %adv_hbm.5, f32[5,5]{1,0:T(8,128)} %coup_hbm.5, f32[5,64,512]{2,1,0:T(8,128)} %state_hbm.3, f32[5,64,512]{2,1,0:T(8,128)} %source_hbm.3, f32[64,512]{1,0:T(8,128)} %visc_hbm.5, ...), custom_call_target="tpu_custom_call", output_to_operand_aliasing={{1}: (5, {})} | custom-call | tf_op jit(solution)/shard_map/pallas_call | solution.py:571
  14.3 0.0 collective-permute-done.1
  14.3 0.4 %collective-permute-start.2 = (f32[200,128]{1,0:T(8,128)S(1)}, f32[200,128]{1,0:T(8,128)S(1)}, u32[]{:S(2)}, u32[]{:S(2)}) collective-permute-start(f32[200,128]{1,0:T(8,128)S(1)} %scatter.10), channel_id=1, source_target_pairs={{0,2},{1,3},{2,0},{3,1},{4,6},{5,7},{6,4},{7,5},{8,10},{9,11},{10,... | collective-permute-start | bytes 307208 | tf_op jit(solution)/shard_map/ppermute | solution.py:513
  14.7 2.7 %collective-permute-done.3 = f32[200,128]{1,0:T(8,128)S(1)} collective-permute-done((f32[200,128]{1,0:T(8,128)S(1)}, f32[200,128]{1,0:T(8,128)S(1)}, u32[]{:S(2)}, u32[]{:S(2)}) %collective-permute-start.3) | collective-permute-done | bytes 102432 | tf_op jit(solution)/shard_map/ppermute | solution.py:513
  17.4 0.6 %collective-permute-start.4 = (f32[200,128]{1,0:T(8,128)S(1)}, f32[200,128]{1,0:T(8,128)S(1)}, u32[]{:S(2)}, u32[]{:S(2)}) collective-permute-start(f32[200,128]{1,0:T(8,128)S(1)} %scatter.11), channel_id=1, source_target_pairs={{0,2},{1,3},{2,0},{3,1},{4,6},{5,7},{6,4},{7,5},{8,10},{9,11},{10,... | collective-permute-start | bytes 307208 | tf_op jit(solution)/shard_map/ppermute | solution.py:513
  18.0 0.0 collective-permute-done.5
  18.0 1.6 %collective-permute-start.6 = (f32[200,128]{1,0:T(8,128)S(1)}, f32[200,128]{1,0:T(8,128)S(1)}, u32[]{:S(2)}, u32[]{:S(2)}) collective-permute-start(f32[200,128]{1,0:T(8,128)S(1)} %scatter.14), channel_id=1, source_target_pairs={{0,2},{1,3},{2,0},{3,1},{4,6},{5,7},{6,4},{7,5},{8,10},{9,11},{10,... | collective-permute-start | bytes 307208 | tf_op jit(solution)/shard_map/ppermute | solution.py:513
  19.6 0.5 %collective-permute-done.2 = f32[200,128]{1,0:T(8,128)S(1)} collective-permute-done((f32[200,128]{1,0:T(8,128)S(1)}, f32[200,128]{1,0:T(8,128)S(1)}, u32[]{:S(2)}, u32[]{:S(2)}) %collective-permute-start.2) | collective-permute-done | bytes 102432 | tf_op jit(solution)/shard_map/ppermute | solution.py:513
  20.2 1.9 %collective-permute-done.4 = f32[200,128]{1,0:T(8,128)S(1)} collective-permute-done((f32[200,128]{1,0:T(8,128)S(1)}, f32[200,128]{1,0:T(8,128)S(1)}, u32[]{:S(2)}, u32[]{:S(2)}) %collective-permute-start.4) | collective-permute-done | bytes 102432 | tf_op jit(solution)/shard_map/ppermute | solution.py:513
  22.1 1.1 %collective-permute-done.6 = f32[200,128]{1,0:T(8,128)S(1)} collective-permute-done((f32[200,128]{1,0:T(8,128)S(1)}, f32[200,128]{1,0:T(8,128)S(1)}, u32[]{:S(2)}, u32[]{:S(2)}) %collective-permute-start.6) | collective-permute-done | bytes 102432 | tf_op jit(solution)/shard_map/ppermute | solution.py:513
  23.2 0.1 collective-permute-start.7
  23.3 2.3 %collective-permute-done.7.odd_ref = f32[1600,128]{1,0:T(8,128)S(1)} collective-permute-done((f32[1600,128]{1,0:T(8,128)S(1)}, f32[1600,128]{1,0:T(8,128)S(1)}, u32[]{:S(2)}, u32[]{:S(2)}) %collective-permute-start.7) | collective-permute-done | bytes 819232 | tf_op jit(solution)/shard_map/ppermute | solution.py:513
  25.6 6.2 %shard_map.93 = f32[5,64,512]{2,1,0:T(8,128)} custom-call(s32[1]{0:T(128)} %bitcast.me_ref, f32[5]{0:T(128)} %adv_hbm.5, f32[5,5]{1,0:T(8,128)} %coup_hbm.5, f32[64,512]{1,0:T(8,128)} %visc_hbm.5, f32[1600,128]{1,0:T(8,128)S(1)} %constant_dynamic-update-slice_fusion.even_ref, ...), custom_call_target="tpu_custom_call", output_to_operand_aliasing={{}: (6, {})} | custom-call | tf_op jit(solution)/shard_map/pallas_call | solution.py:611
  (12 shorter events, 0.2 us)
Async XLA Ops:
  2.3 7.4 %collective-permute-start = (f32[200,128]{1,0:T(8,128)S(1)}, f32[200,128]{1,0:T(8,128)S(1)}, u32[]{:S(2)}, u32[]{:S(2)}) collective-permute-start(f32[200,128]{1,0:T(8,128)S(1)} %shard_map.91), channel_id=1, source_target_pairs={{0,2},{1,3},{2,0},{3,1},{4,6},{5,7},{6,4},{7,5},{8,10},{9,11},{10,... | collective-permute-start | bytes 307208 | tf_op jit(solution)/shard_map/ppermute | solution.py:513
  5.4 8.9 %collective-permute-start.1 = (f32[200,128]{1,0:T(8,128)S(1)}, f32[200,128]{1,0:T(8,128)S(1)}, u32[]{:S(2)}, u32[]{:S(2)}) collective-permute-start(f32[200,128]{1,0:T(8,128)S(1)} %shard_map.91), channel_id=1, source_target_pairs={{0,4},{1,5},{2,6},{3,7},{4,0},{5,1},{6,2},{7,3},{8,12},{9,13},{10,... | collective-permute-start | bytes 307208 | tf_op jit(solution)/shard_map/ppermute | solution.py:513
  6.9 10.4 %collective-permute-start.3 = (f32[200,128]{1,0:T(8,128)S(1)}, f32[200,128]{1,0:T(8,128)S(1)}, u32[]{:S(2)}, u32[]{:S(2)}) collective-permute-start(f32[200,128]{1,0:T(8,128)S(1)} %shard_map.91), channel_id=1, source_target_pairs={{0,8},{1,9},{2,10},{3,11},{4,12},{5,13},{6,14},{7,15},{8,0},{9,1},... | collective-permute-start | bytes 307208 | tf_op jit(solution)/shard_map/ppermute | solution.py:513
  9.5 8.5 %collective-permute-start.5 = (f32[200,128]{1,0:T(8,128)S(1)}, f32[200,128]{1,0:T(8,128)S(1)}, u32[]{:S(2)}, u32[]{:S(2)}) collective-permute-start(f32[200,128]{1,0:T(8,128)S(1)} %shard_map.91), channel_id=1, source_target_pairs={{0,12},{1,13},{2,14},{3,15},{4,8},{5,9},{6,10},{7,11},{8,4},{9,5},... | collective-permute-start | bytes 307208 | tf_op jit(solution)/shard_map/ppermute | solution.py:513
  14.3 5.8 %collective-permute-start.2 = (f32[200,128]{1,0:T(8,128)S(1)}, f32[200,128]{1,0:T(8,128)S(1)}, u32[]{:S(2)}, u32[]{:S(2)}) collective-permute-start(f32[200,128]{1,0:T(8,128)S(1)} %scatter.10), channel_id=1, source_target_pairs={{0,2},{1,3},{2,0},{3,1},{4,6},{5,7},{6,4},{7,5},{8,10},{9,11},{10,... | collective-permute-start | bytes 307208 | tf_op jit(solution)/shard_map/ppermute | solution.py:513
  17.4 4.7 %collective-permute-start.4 = (f32[200,128]{1,0:T(8,128)S(1)}, f32[200,128]{1,0:T(8,128)S(1)}, u32[]{:S(2)}, u32[]{:S(2)}) collective-permute-start(f32[200,128]{1,0:T(8,128)S(1)} %scatter.11), channel_id=1, source_target_pairs={{0,2},{1,3},{2,0},{3,1},{4,6},{5,7},{6,4},{7,5},{8,10},{9,11},{10,... | collective-permute-start | bytes 307208 | tf_op jit(solution)/shard_map/ppermute | solution.py:513
  18.0 5.2 %collective-permute-start.6 = (f32[200,128]{1,0:T(8,128)S(1)}, f32[200,128]{1,0:T(8,128)S(1)}, u32[]{:S(2)}, u32[]{:S(2)}) collective-permute-start(f32[200,128]{1,0:T(8,128)S(1)} %scatter.14), channel_id=1, source_target_pairs={{0,2},{1,3},{2,0},{3,1},{4,6},{5,7},{6,4},{7,5},{8,10},{9,11},{10,... | collective-permute-start | bytes 307208 | tf_op jit(solution)/shard_map/ppermute | solution.py:513
  23.2 2.4 %collective-permute-start.7 = (f32[1600,128]{1,0:T(8,128)S(1)}, f32[1600,128]{1,0:T(8,128)S(1)}, u32[]{:S(2)}, u32[]{:S(2)}) collective-permute-start(f32[1600,128]{1,0:T(8,128)S(1)} %constant_dynamic-update-slice_fusion.even_ref), channel_id=1, source_target_pairs={{0,1},{1,0},{2,3},{3,2},{4,5},{5,4},{6,7},{7,6},{8,9},{9,8},{10,11... | collective-permute-start | bytes 2457608 | tf_op jit(solution)/shard_map/ppermute | solution.py:513
